TPU v7x, 32 devices: a whole 2x2x4 slice. The times are simulated.
32 devices in a mesh: ctx: 4 (over x, core), tp: 8 (over z, y).
Axes of the slice: x: 2, y: 2, z: 4, core: 2. Of those that a mesh axis runs over, the one named last changes fastest.
Arguments:
- out_grad: bfloat16 [4096, 4096], P('ctx', 'tp'), may hold values from -6 to 6
- pre_act: bfloat16 [4096, 4096], P('ctx', 'tp'), may hold values from -6 to 6
- normed: bfloat16 [4096, 12800], P('ctx', 'tp'), may hold values from -5 to 5
- inverse_std: float32 [4096], P('ctx'), may hold values from 0.5 to 2
- w_up: bfloat16 [4096, 12800], P(None, 'tp')
- w_down: bfloat16 [4096, 4096], P(None, 'tp'), may hold values from -0.09375 to 0.09375
- ln_gain: float32 [12800], P('tp'), may hold values from 0.25 to 1.75
- owner_map: int32 [4, 4], P('ctx'), may hold values from 0 to 7, as said below
Outputs:
- grad_w2: float32 [4096, 4096], P('ctx', 'tp')
- grad_w1: float32 [4096, 12800], P('ctx', 'tp')
- grad_b1: float32 [4096], P('tp')
- grad_b2: float32 [4096], P('tp')
- ln_grads: float32 [2, 12800], P(None, 'tp')
- vit_grad: bfloat16 [8192, 12800], P(('ctx', 'tp'))
Inputs may be any that keep to these rules, and one draw needn't show every extreme that they name: `owner_map`: within each context shard, every encoder rank owns at most 1 of the 4 images, and some rank owns exactly 1.
All inputs are finite; a program needn't handle non-finite values.
Results may differ from a plain program's by a relative error of at most 0.007.
Values may be sent and summed in bfloat16 or wider, within the bound.
No kernel may reach another device: no remote copies, remote signals or barrier semaphores. Data moves between devices by JAX's collectives and lax.ppermute only.
A program may use at most 192 MiB of HBM per device.

v0:
```python
import functools
import math

import jax
import jax.numpy as jnp
from jax import lax
from jax.experimental import pallas as pl
from jax.experimental.pallas import tpu as pltpu
from jax.sharding import PartitionSpec as P

CHUNKS = 2
VMEM_LIMIT = 48 * 1024 * 1024


def gelu_parts(linear):
    normal_cdf = 0.5 * (1.0 + jax.scipy.special.erf(linear * 2.0 ** (-0.5)))
    density = jnp.exp(-0.5 * linear * linear) * (2.0 * math.pi) ** (-0.5)
    return (linear * normal_cdf, normal_cdf + linear * density)


def slot_numbers(owners, capacity):
    position = jnp.arange(owners.shape[0])
    earlier = (owners[None, :] == owners[:, None]) & (position[None, :] < position[:, None])
    return owners * capacity + jnp.sum(earlier.astype(jnp.int32), axis=1)


def divisor(extent, most, unit):
    return max(d for d in range(unit, most + 1, unit) if extent % d == 0)


def ring_order(count):
    depth = 4 if count % 4 == 0 else count
    width = count // depth
    walk = [(z, 0) for z in range(depth)]
    if width > 1:
        for turn, z in enumerate(reversed(range(depth))):
            ys = list(range(1, width))
            walk += [(z, y) for y in (ys if turn % 2 == 0 else ys[::-1])]
    return [z * width + y for z, y in walk]


def ring_owners(count):
    order = ring_order(count)
    table = []
    for j in range(count):
        at = order.index(j)
        steps = [0]
        for step in range(1, count // 2):
            steps += [-step, step]
        steps += [count // 2]
        table.append([order[(at + s) % count] for s in steps])
    core = (lax.axis_index("ctx") % 2).astype(jnp.int32)
    return jnp.concatenate([jnp.array(table, jnp.int32)[lax.axis_index("tp")], core[None]])


def ring_blocks(block, count):
    order = ring_order(count)
    ahead = [(order[p], order[(p + 1) % count]) for p in range(count)]
    behind = [(order[p], order[(p - 1) % count]) for p in range(count)]
    up, down = block, block
    blocks = [block]
    for _ in range(1, count // 2):
        up = lax.ppermute(up, "tp", ahead)
        down = lax.ppermute(down, "tp", behind)
        blocks += [up, down]
    half = block.shape[0] // 2
    blocks.append(lax.ppermute(up[:half], "tp", ahead))
    blocks.append(lax.ppermute(down[half:], "tp", behind))
    return blocks


def assemble(owners_ref, block_refs, held, sems):
    rows, width = block_refs[0].shape
    half = rows // 2
    last = len(block_refs) - 2
    copies = []
    for k, ref in enumerate(block_refs):
        columns = pl.ds(pl.multiple_of(owners_ref[min(k, last)] * width, width), width)
        if k < last:
            target = held.at[:, columns]
        else:
            target = held.at[pl.ds((k - last) * half, half), columns]
        copies.append(pltpu.make_async_copy(ref, target, sems.at[k]))
    return copies


def spread(ring_ref, held, full_ref, swap_ref, chunk, image_rows, sems):
    rows, part_rows = held.shape[0], image_rows // CHUNKS
    all_rows, member_width = full_ref.shape[0], swap_ref.shape[1]
    other = 1 - ring_ref[ring_ref.shape[0] - 1]
    copies = []
    for i in range(rows // part_rows):
        source = pl.ds(i * part_rows, part_rows)
        place = i * image_rows + chunk * part_rows
        copies.append((held.at[source, :], full_ref.at[pl.ds(place, part_rows), :]))
        for chip in range(swap_ref.shape[0] // all_rows):
            columns = pl.ds(
                pl.multiple_of((2 * chip + other) * member_width, member_width), member_width
            )
            target = swap_ref.at[pl.ds(chip * all_rows + place, part_rows), :]
            copies.append((held.at[source, columns], target))
    return [
        pltpu.make_async_copy(source, target, sems.at[n])
        for n, (source, target) in enumerate(copies)
    ]


def spread_shapes(rows, chunk_rows, full, ctx_count, images):
    shapes = (
        jax.ShapeDtypeStruct((rows, full), jnp.bfloat16),
        jax.ShapeDtypeStruct((rows * (ctx_count // 2), full // ctx_count), jnp.bfloat16),
    )
    scratch = [
        pltpu.VMEM((chunk_rows, full), jnp.bfloat16),
        pltpu.SemaphoreType.DMA((2 * tp_most(),)),
        pltpu.SemaphoreType.DMA((images * (1 + ctx_count // 2),)),
    ]
    return shapes, scratch


def tp_most():
    return lax.axis_size("tp")


def back_kernel(chunk, image_rows, blocks, carried, ring_ref, *refs):
    block_refs, refs = refs[:blocks], refs[blocks:]
    w_ref, slope_ref, *refs = refs
    back_ref, sum_ref, full_ref, swap_ref, held, sems, out_sems = refs[carried:]
    copies = assemble(ring_ref, block_refs, held, sems)
    for copy in copies:
        copy.start()
    for copy in copies:
        copy.wait()
    outs = spread(ring_ref, held, full_ref, swap_ref, chunk, image_rows, out_sems)
    for copy in outs:
        copy.start()
    rows, part_rows = held.shape[0], image_rows // CHUNKS
    tile = divisor(rows, 256, part_rows)
    sums = jnp.zeros(sum_ref.shape, jnp.float32)
    for start in range(0, rows, tile):
        total = jnp.dot(
            held[start : start + tile, :], w_ref[...], preferred_element_type=jnp.float32
        )
        for n in range(tile // part_rows):
            image = start // part_rows + n
            place = image * image_rows + chunk * part_rows
            part = (
                total[n * part_rows : (n + 1) * part_rows]
                * slope_ref[place : place + part_rows, :]
            ).astype(back_ref.dtype)
            back_ref[image * part_rows : (image + 1) * part_rows, :] = part
            sums += jnp.sum(part.astype(jnp.float32), axis=0, keepdims=True)
    sum_ref[...] = sums
    for copy in outs:
        copy.wait()


def back_part(ring, blocks, w_down, slope, chunk, image_rows, ctx_count, so_far):
    rows = blocks[0].shape[0]
    full, width = w_down.shape
    images = slope.shape[0] // image_rows
    shapes, scratch = spread_shapes(slope.shape[0], rows, full, ctx_count, images)
    first = 1 + len(blocks) + 2
    return pl.pallas_call(
        functools.partial(back_kernel, chunk, image_rows, len(blocks), len(so_far)),
        out_shape=(
            jax.ShapeDtypeStruct((rows, width), jnp.bfloat16),
            jax.ShapeDtypeStruct((1, width), jnp.float32),
        )
        + shapes,
        in_specs=[pl.BlockSpec(memory_space=pltpu.SMEM)]
        + [pl.BlockSpec(memory_space=pl.ANY)] * len(blocks)
        + [pl.BlockSpec(memory_space=pltpu.VMEM)] * 2
        + [pl.BlockSpec(memory_space=pltpu.HBM)] * len(so_far),
        out_specs=(pl.BlockSpec(memory_space=pltpu.VMEM),) * 2
        + (pl.BlockSpec(memory_space=pltpu.HBM),) * 2,
        scratch_shapes=scratch,
        input_output_aliases={first + n: 2 + n for n in range(len(so_far))},
        compiler_params=pltpu.CompilerParams(vmem_limit_bytes=VMEM_LIMIT),
        cost_estimate=pl.CostEstimate(
            flops=2 * rows * full * width,
            bytes_accessed=2 * (2 * rows * full + full * width),
            transcendentals=0,
        ),
    )(ring, *blocks, w_down, slope, *so_far)


def norm_kernel(chunk, image_rows, blocks, images, carried, ring_ref, *refs):
    block_refs, refs = refs[:blocks], refs[blocks:]
    w_ref, gain_ref, *refs = refs
    normed_refs, refs = refs[:images], refs[images:]
    gained_ref, sums_ref, ln_ref, full_ref, swap_ref, held, sems, out_sems = refs[carried:]
    step = pl.program_id(0)
    outs = spread(ring_ref, held, full_ref, swap_ref, chunk, image_rows, out_sems)

    @pl.when(step == 0)
    def _():
        copies = assemble(ring_ref, block_refs, held, sems)
        for copy in copies:
            copy.start()
        for copy in copies:
            copy.wait()
        for copy in outs:
            copy.start()
        sums_ref[...] = jnp.zeros_like(sums_ref)

    grad = lax.dot_general(
        w_ref[...], held[...], (((1,), (1,)), ((), ())), preferred_element_type=jnp.float32
    )
    features = jnp.concatenate([ref[...] for ref in normed_refs], axis=1).astype(jnp.float32)
    gained = gain_ref[...] * grad
    gained_ref[...] = gained
    sums_ref[0:1, :] += jnp.sum(gained, axis=0, keepdims=True)
    sums_ref[1:2, :] += jnp.sum(gained * features, axis=0, keepdims=True)
    gains = jnp.sum(grad * features, axis=1, keepdims=True)
    biases = jnp.sum(grad, axis=1, keepdims=True)
    lane = lax.broadcasted_iota(jnp.int32, ln_ref.shape, 1)
    ln_ref[...] = jnp.where(lane == 0, gains, biases)

    @pl.when(step == pl.num_programs(0) - 1)
    def _():
        for copy in outs:
            copy.wait()


def norm_part(ring, blocks, w_up_t, gain, normed_t, chunk, image_rows, ctx_count, so_far, after):
    rows = blocks[0].shape[0]
    width, full = w_up_t.shape
    part_rows = image_rows // CHUNKS
    images = rows // part_rows
    tile = divisor(width, 400, 16)
    shapes, scratch = spread_shapes(normed_t.shape[1], rows, full, ctx_count, images)
    first = 1 + len(blocks) + 2 + images
    return pl.pallas_call(
        functools.partial(
            norm_kernel, chunk, image_rows, len(blocks), images, len(so_far) + len(after)
        ),
        grid=(width // tile,),
        out_shape=(
            jax.ShapeDtypeStruct((width, rows), jnp.float32),
            jax.ShapeDtypeStruct((2, rows), jnp.float32),
            jax.ShapeDtypeStruct((width, 128), jnp.float32),
        )
        + shapes,
        in_specs=[pl.BlockSpec(memory_space=pltpu.SMEM)]
        + [pl.BlockSpec(memory_space=pl.ANY)] * len(blocks)
        + [
            pl.BlockSpec((tile, full), lambda t: (t, 0)),
            pl.BlockSpec((tile, 1), lambda t: (t, 0)),
        ]
        + [
            pl.BlockSpec((tile, part_rows), lambda t, i=i: (t, i * CHUNKS + chunk))
            for i in range(images)
        ]
        + [pl.BlockSpec(memory_space=pltpu.HBM)] * (len(so_far) + len(after)),
        out_specs=(
            pl.BlockSpec((tile, rows), lambda t: (t, 0)),
            pl.BlockSpec((2, rows), lambda t: (0, 0)),
            pl.BlockSpec((tile, 128), lambda t: (t, 0)),
        )
        + (pl.BlockSpec(memory_space=pltpu.HBM),) * 2,
        scratch_shapes=scratch,
        input_output_aliases={first + n: 3 + n for n in range(len(so_far))},
        compiler_params=pltpu.CompilerParams(vmem_limit_bytes=VMEM_LIMIT),
        cost_estimate=pl.CostEstimate(
            flops=2 * rows * full * width,
            bytes_accessed=2 * (full * width + 2 * rows * full) + 6 * rows * width,
            transcendentals=0,
        ),
    )(ring, *blocks, w_up_t, gain, *[normed_t] * images, *so_far, *after)


def pair_kernel(
    contract, scale, ranges, member_ref, a_ref, a_other_ref, b_ref, b_other_ref, *refs
):
    arrived, out_ref = refs[: len(ranges)], refs[-1]
    dims = (contract, ((), ()))
    total = lax.dot_general(a_ref[...], b_ref[...], dims, preferred_element_type=jnp.float32)
    total += lax.dot_general(
        a_other_ref[...], b_other_ref[...], dims, preferred_element_type=jnp.float32
    )
    total *= scale
    step = pl.program_id(0)
    for (first, last), ref in zip(ranges, arrived):
        part = ref[...].astype(jnp.float32)
        total += jnp.where((step >= first) & (step < last), part, 0.0)
    out_ref[...] = total.astype(out_ref.dtype)


def pair_product(
    operands, specs, contract, shape, tile, depth, member, scale, arrived, dtype, after
):
    row_spec = lambda first, last: pl.BlockSpec(
        (tile, shape[1]), lambda t, m: (jnp.clip(t - first, 0, last - first - 1), 0)
    )
    steps = shape[0] // tile
    return pl.pallas_call(
        functools.partial(pair_kernel, contract, scale, [span for span, _ in arrived]),
        grid_spec=pltpu.PrefetchScalarGridSpec(
            num_scalar_prefetch=1,
            grid=(steps,),
            in_specs=specs
            + [row_spec(*span) for span, _ in arrived]
            + [pl.BlockSpec(memory_space=pltpu.HBM)] * len(after),
            out_specs=row_spec(0, steps),
        ),
        out_shape=jax.ShapeDtypeStruct(shape, dtype),
        compiler_params=pltpu.CompilerParams(vmem_limit_bytes=VMEM_LIMIT),
        cost_estimate=pl.CostEstimate(
            flops=4 * shape[0] * shape[1] * depth,
            bytes_accessed=4 * depth * (shape[0] + shape[1]) + 4 * shape[0] * shape[1],
            transcendentals=0,
        ),
    )(
        member.reshape(1).astype(jnp.int32),
        *operands,
        *[part for _, part in arrived],
        *after,
    )


def chip_products(product, spans, ctx_count, after):
    index = lax.axis_index("ctx")
    going, arrived = [], []
    for span in spans:
        for shift in range(1, ctx_count // 2):
            member = (index + 2 * shift) % ctx_count
            going.append(product(member, span, [], jnp.bfloat16, after))
            route = [(c, (c + 2 * shift) % ctx_count) for c in range(ctx_count)]
            arrived.append((span, lax.ppermute(going[-1], "ctx", route)))
    return going, arrived


def tie_kernel(*refs):
    del refs


def tie(values, others):
    return pl.pallas_call(
        tie_kernel,
        in_specs=[pl.BlockSpec(memory_space=pl.ANY)] * (len(values) + len(others)),
        out_specs=[pl.BlockSpec(memory_space=pl.ANY)] * len(values),
        out_shape=[jax.ShapeDtypeStruct(value.shape, value.dtype) for value in values],
        input_output_aliases={n: n for n in range(len(values))},
        compiler_params=pltpu.CompilerParams(vmem_limit_bytes=VMEM_LIMIT),
    )(*values, *others)


def visual_kernel(
    source_ref, present_ref, gained_ref, normed_ref, means_ref, inverse_ref, out_ref
):
    slot = pl.program_id(0)

    @pl.when(present_ref[slot] == 0)
    def _():
        out_ref[...] = jnp.zeros_like(out_ref)

    @pl.when(present_ref[slot] != 0)
    def _():
        gained = gained_ref[...]
        features = normed_ref[...].astype(jnp.float32)
        first, second = means_ref[0:1, :], means_ref[1:2, :]
        out_ref[0] = (inverse_ref[...] * (gained - first - features * second)).astype(
            out_ref.dtype
        )


def visual_slots(source, present, gained_t, normed_t, means, inverse, chunk, part_rows):
    width = gained_t.shape[0]
    slots = source.shape[0]
    picked = lambda s, source, present: (0, source[s])
    natural = lambda s, source, present: (0, source[s] * CHUNKS + chunk)
    return pl.pallas_call(
        visual_kernel,
        grid_spec=pltpu.PrefetchScalarGridSpec(
            num_scalar_prefetch=2,
            grid=(slots,),
            in_specs=[
                pl.BlockSpec((width, part_rows), picked),
                pl.BlockSpec((width, part_rows), natural),
                pl.BlockSpec((2, part_rows), picked),
                pl.BlockSpec((1, part_rows), natural),
            ],
            out_specs=pl.BlockSpec((1, width, part_rows), lambda s, source, present: (s, 0, 0)),
        ),
        out_shape=jax.ShapeDtypeStruct((slots, width, part_rows), jnp.bfloat16),
        compiler_params=pltpu.CompilerParams(vmem_limit_bytes=VMEM_LIMIT),
        cost_estimate=pl.CostEstimate(
            flops=6 * slots * width * part_rows,
            bytes_accessed=8 * slots * width * part_rows,
            transcendentals=0,
        ),
    )(source, present, gained_t, normed_t, means, inverse)


def turn_kernel(in_ref, *refs):
    refs[-1][...] = in_ref[...].T


def turn_rows(received, chunk, rows, so_far, after):
    full, part_rows = received.shape
    tile = divisor(full, 2560, 128)
    operands, aliases = [received], {}
    if so_far is not None:
        operands.append(so_far)
        aliases = {1: 0}
    operands += after
    specs = [pl.BlockSpec((tile, part_rows), lambda t: (t, 0))]
    specs += [pl.BlockSpec(memory_space=pltpu.HBM)] * (len(operands) - 1)
    return pl.pallas_call(
        turn_kernel,
        grid=(full // tile,),
        in_specs=specs,
        out_specs=pl.BlockSpec((part_rows, tile), lambda t: (chunk, t)),
        out_shape=jax.ShapeDtypeStruct((rows, full), received.dtype),
        input_output_aliases=aliases,
        compiler_params=pltpu.CompilerParams(vmem_limit_bytes=VMEM_LIMIT),
        cost_estimate=pl.CostEstimate(
            flops=0, bytes_accessed=4 * part_rows * full, transcendentals=0
        ),
    )(*operands)


def core_swap(value, ctx_count):
    return lax.ppermute(value, "ctx", [(c, c ^ 1) for c in range(ctx_count)])


def doubling_sum(value, axis, count, after=()):
    bit = 1
    while bit < count:
        if after and 2 * bit >= count:
            (value,) = tie([value], after)
        value = value + lax.ppermute(value, axis, [(t, t ^ bit) for t in range(count)])
        bit *= 2
    return value


def per_device(out_grad, pre_act, normed, inverse_std, w_up, w_down, ln_gain, owner_map):
    ctx_count = lax.axis_size("ctx")
    tp_count = lax.axis_size("tp")
    row_count = out_grad.shape[0]
    width = normed.shape[1]
    grad_scale = float(row_count * ctx_count) ** (-0.5)
    full_width = float(width * tp_count)

    owners = owner_map[0]
    image_count = owners.shape[0]
    image_rows = row_count // image_count
    part_rows = image_rows // CHUNKS
    chunk_rows = row_count // CHUNKS
    capacity = max(1, 2 * image_count // tp_count)
    slot_of = slot_numbers(owners, capacity)
    slot_ids = jnp.arange(tp_count * capacity)
    matches = slot_of[None, :] == slot_ids[:, None]
    present = jnp.any(matches, axis=1).astype(jnp.int32)
    source = jnp.sum(jnp.where(matches, jnp.arange(image_count)[None, :], 0), axis=1).astype(
        jnp.int32
    )

    def chunk_of(array, chunk):
        images = array.reshape((image_count, image_rows) + array.shape[1:])
        piece = images[:, chunk * part_rows : (chunk + 1) * part_rows]
        return piece.reshape((chunk_rows,) + array.shape[1:])

    ring = ring_owners(tp_count)
    gelu_value, slope = gelu_parts(pre_act.astype(jnp.float32))
    hidden = gelu_value.astype(jnp.bfloat16)
    hidden_other = core_swap(hidden, ctx_count)
    normed_t = normed.T
    normed_other = core_swap(normed_t, ctx_count)
    gain = ln_gain[:, None]
    w_up_t = w_up.T

    def back_of(chunk, blocks, so_far):
        return back_part(ring, blocks, w_down, slope, chunk, image_rows, ctx_count, so_far)

    first_grads, second_grads = [
        ring_blocks(chunk_of(out_grad, chunk), tp_count) for chunk in range(CHUNKS)
    ]
    first_back, first_sum, *so_far = back_of(0, first_grads, ())
    first_backs = ring_blocks(first_back, tp_count)
    second_back, second_sum, grads, grads_swap = back_of(1, second_grads, so_far)
    second_backs = ring_blocks(second_back, tp_count)
    grads_other = core_swap(grads_swap, ctx_count)
    back_sum = first_sum[0] + second_sum[0]

    def grad_w2_share(member, span, arrived, dtype, after):
        share, local = grads.shape[1] // ctx_count, hidden.shape[1]
        tile = divisor(share, 256, 128)
        steps = share // tile
        return pair_product(
            (grads, grads_other, hidden, hidden_other),
            [
                pl.BlockSpec((row_count, tile), lambda t, m: (0, m[0] * steps + t)),
                pl.BlockSpec((row_count, tile), lambda t, m: (m[0] // 2, t)),
                pl.BlockSpec((row_count, local), lambda t, m: (0, 0)),
                pl.BlockSpec((row_count, local), lambda t, m: (0, 0)),
            ],
            ((0,), (0,)), (share, local), tile, row_count, member, grad_scale, arrived, dtype,
            after,
        )

    w2_span = (0, grads.shape[1] // ctx_count // divisor(grads.shape[1] // ctx_count, 256, 128))
    going_w2, arrived_w2 = chip_products(grad_w2_share, [w2_span], ctx_count, [])
    member = lax.axis_index("ctx")

    def norm_of(chunk, blocks, so_far, after):
        return norm_part(
            ring, blocks, w_up_t, gain, normed_t, chunk, image_rows, ctx_count, so_far, after
        )

    def slots_of(chunk, gained_t, means):
        return visual_slots(
            source, present, gained_t, normed_t, means, inverse_std[None, :], chunk, part_rows
        )

    first_gained, first_rows, first_ln, *so_far = norm_of(0, first_backs, (), [])
    first_means = doubling_sum(first_rows, "tp", tp_count) / full_width
    first_slots, first_means = tie(
        [slots_of(0, first_gained, first_means), first_means], second_backs[-2:]
    )
    outgoing = [first_slots]
    second_gained, second_rows, second_ln, backs, backs_swap = norm_of(
        1, second_backs, so_far, [first_means]
    )
    backs_other = core_swap(backs_swap, ctx_count)

    w1_tile = divisor(width, 400, 16)
    w1_tiles = width // w1_tile

    def grad_w1_share(member, span, arrived, dtype, after):
        share = backs.shape[1] // ctx_count
        first, last = span
        return pair_product(
            (normed_t, normed_other, backs, backs_other),
            [
                pl.BlockSpec((w1_tile, row_count), lambda t, m: (first + t, 0)),
                pl.BlockSpec((w1_tile, row_count), lambda t, m: (first + t, 0)),
                pl.BlockSpec((row_count, share), lambda t, m: (0, m[0])),
                pl.BlockSpec((row_count, share), lambda t, m: (m[0] // 2, 0)),
            ],
            ((1,), (0,)), ((last - first) * w1_tile, share), w1_tile, row_count, member,
            grad_scale, arrived, dtype, after,
        )

    cut = w1_tiles // 2
    spans = [(0, cut), (cut, w1_tiles)] if cut else [(0, w1_tiles)]
    going_w1, arrived_w1 = chip_products(grad_w1_share, spans, ctx_count, going_w2)

    second_means = doubling_sum(second_rows, "tp", tp_count, going_w1) / full_width
    early = [part for span, part in arrived_w1 if span == spans[0]]
    outgoing += tie([slots_of(1, second_gained, second_means)], early)
    received = [
        lax.all_to_all(part, "tp", split_axis=0, concat_axis=0, tiled=True) for part in outgoing
    ]
    ln_sum = (first_ln + second_ln)[:, :2]
    small = jnp.concatenate(
        [jnp.sum(out_grad.astype(jnp.float32), axis=0), back_sum, ln_sum.T.reshape(-1)]
    )
    (small,) = tie([small], [part for _, part in arrived_w1])
    grad_w2 = grad_w2_share(member, w2_span, arrived_w2, jnp.float32, [small])
    small = doubling_sum(small, "ctx", ctx_count) * grad_scale
    grad_w1_t = grad_w1_share(member, (0, w1_tiles), arrived_w1, jnp.float32, [])
    assert capacity == 1
    vit_grad = None
    for chunk in range(CHUNKS):
        columns = received[chunk].reshape(tp_count * width, part_rows)
        after = [grad_w1_t, grad_w2] if chunk + 1 == CHUNKS else []
        vit_grad = turn_rows(columns, chunk, image_rows, vit_grad, after)

    features_in = out_grad.shape[1]
    hidden_in = pre_act.shape[1]
    bias_down = small[:features_in]
    bias_up = small[features_in : features_in + hidden_in]
    ln_grads = small[features_in + hidden_in :].reshape(2, width)
    return (grad_w2, grad_w1_t.T, bias_up, bias_down, ln_grads, vit_grad)


def solution(mesh):
    return jax.shard_map(
        per_device,
        mesh=mesh,
        in_specs=(
            P("ctx", "tp"),
            P("ctx", "tp"),
            P("ctx", "tp"),
            P("ctx"),
            P(None, "tp"),
            P(None, "tp"),
            P("tp"),
            P("ctx", None),
        ),
        out_specs=(
            P("ctx", "tp"),
            P("ctx", "tp"),
            P("tp"),
            P("tp"),
            P(None, "tp"),
            P(("ctx", "tp"), None),
        ),
        check_vma=False,
    )
```

profile of v0, /device:TPU:0, one launch (start us, length us, event | category | flops | bytes accessed | tf_op | source)
XLA Modules:
  0.0 371.5 jit_solution(6508307055792903036)
XLA Ops:
  1.9 3.1 collective-permute-start.8
  5.0 11.9 %collective-permute-done.8.refs_1_ = bf16[512,512]{1,0:T(8,128)(2,1)S(1)} collective-permute-done((bf16[512,512]{1,0:T(8,128)(2,1)S(1)}, bf16[512,512]{1,0:T(8,128)(2,1)S(1)}, u32[]{:S(2)}, u32[]{:S(2)}) %collective-permute-start.8) | collective-permute-done | bytes 524320 | tf_op jit(solution)/shard_map/ppermute | solution.py:63
  16.9 1.8 collective-permute-start.10
  20.5 1.8 collective-permute-start
  22.5 9.3 %collective-permute-done.10.refs_3_ = bf16[512,512]{1,0:T(8,128)(2,1)} collective-permute-done((bf16[512,512]{1,0:T(8,128)(2,1)S(1)}, bf16[512,512]{1,0:T(8,128)(2,1)}, u32[]{:S(2)}, u32[]{:S(2)}) %collective-permute-start.10) | collective-permute-done | bytes 524320 | tf_op jit(solution)/shard_map/ppermute | solution.py:63
  31.9 1.8 collective-permute-start.12
  34.7 8.3 %collective-permute-done.refs_1_ = bf16[512,512]{1,0:T(8,128)(2,1)S(1)} collective-permute-done((bf16[512,512]{1,0:T(8,128)(2,1)S(1)}, bf16[512,512]{1,0:T(8,128)(2,1)S(1)}, u32[]{:S(2)}, u32[]{:S(2)}) %collective-permute-start) | collective-permute-done | bytes 524320 | tf_op jit(solution)/shard_map/ppermute | solution.py:63
  43.0 1.8 collective-permute-start.2
  46.6 7.6 %collective-permute-done.12.refs_5_ = bf16[512,512]{1,0:T(8,128)(2,1)S(1)} collective-permute-done((bf16[512,512]{1,0:T(8,128)(2,1)}, bf16[512,512]{1,0:T(8,128)(2,1)S(1)}, u32[]{:S(2)}, u32[]{:S(2)}) %collective-permute-start.12) | collective-permute-done | bytes 524320 | tf_op jit(solution)/shard_map/ppermute | solution.py:63
  54.2 1.8 collective-permute-start.14
  57.1 3.2 fusion.6
  60.3 5.2 %collective-permute-done.2.refs_3_ = bf16[512,512]{1,0:T(8,128)(2,1)S(1)} collective-permute-done((bf16[512,512]{1,0:T(8,128)(2,1)S(1)}, bf16[512,512]{1,0:T(8,128)(2,1)S(1)}, u32[]{:S(2)}, u32[]{:S(2)}) %collective-permute-start.2) | collective-permute-done | bytes 524320 | tf_op jit(solution)/shard_map/ppermute | solution.py:63
  68.3 2.8 collective-permute-done.14.refs_7_
  71.1 2.6 collective-permute-done.15.refs_8_
  73.7 7.2 %shard_map.136 = (bf16[512,512]{1,0:T(8,128)(2,1)S(1)}, f32[1,512]{1,0:T(1,128)S(1)}, bf16[1024,4096]{1,0:T(8,128)(2,1)}, bf16[2048,1024]{1,0:T(8,128)(2,1)}) custom-call(s32[9]{0:T(128)S(1)} %pad_add_fusion.ring_ref, bf16[512,512]{1,0:T(8,128)(2,1)S(1)} %bitcast.44, bf16[512,512]{1,0:T(8,128)(2,1)S(1)} %copy-done.12, bf16[512,512]{1,0:T(8,128)(2,1)S(1)} %copy-done.14, ...), custom_call_target="tpu_custom_call" | custom-call | flops 2147483648 | bytes 12582912 | tf_op jit(solution)/shard_map/pallas_call | solution.py:164
  85.2 10.6 %collective-permute-done.19.refs_1_ = bf16[512,512]{1,0:T(8,128)(2,1)S(1)} collective-permute-done((bf16[512,512]{1,0:T(8,128)(2,1)S(1)}, bf16[512,512]{1,0:T(8,128)(2,1)S(1)}, u32[]{:S(2)}, u32[]{:S(2)}) %collective-permute-start.19) | collective-permute-done | bytes 524320 | tf_op jit(solution)/shard_map/ppermute | solution.py:63
  97.8 3.6 collective-permute-done.6.refs_7_
  103.0 6.4 %shard_map.137 = (bf16[512,512]{1,0:T(8,128)(2,1)S(1)}, f32[1,512]{1,0:T(1,128)S(1)}, bf16[1024,4096]{1,0:T(8,128)(2,1)}, bf16[2048,1024]{1,0:T(8,128)(2,1)}) custom-call(s32[9]{0:T(128)S(1)} %pad_add_fusion.ring_ref, bf16[512,512]{1,0:T(8,128)(2,1)S(1)} %bitcast.41, ...), custom_call_target="tpu_custom_call", output_to_operand_aliasing={{2}: (12, {}), {3}: (13, {})} | custom-call | flops 2147483648 | bytes 12582912 | tf_op jit(solution)/shard_map/pallas_call | solution.py:164
  114.7 9.6 %collective-permute-done.27.refs_1_ = bf16[512,512]{1,0:T(8,128)(2,1)S(1)} collective-permute-done((bf16[512,512]{1,0:T(8,128)(2,1)S(1)}, bf16[512,512]{1,0:T(8,128)(2,1)S(1)}, u32[]{:S(2)}, u32[]{:S(2)}) %collective-permute-start.27) | collective-permute-done | bytes 524320 | tf_op jit(solution)/shard_map/ppermute | solution.py:63
  126.4 9.2 %collective-permute-done.23.refs_5_ = bf16[512,512]{1,0:T(8,128)(2,1)S(1)} collective-permute-done((bf16[512,512]{1,0:T(8,128)(2,1)S(1)}, bf16[512,512]{1,0:T(8,128)(2,1)S(1)}, u32[]{:S(2)}, u32[]{:S(2)}) %collective-permute-start.23) | collective-permute-done | bytes 524320 | tf_op jit(solution)/shard_map/ppermute | solution.py:63
  138.2 8.6 %collective-permute-done.29.refs_3_ = bf16[512,512]{1,0:T(8,128)(2,1)S(1)} collective-permute-done((bf16[512,512]{1,0:T(8,128)(2,1)S(1)}, bf16[512,512]{1,0:T(8,128)(2,1)S(1)}, u32[]{:S(2)}, u32[]{:S(2)}) %collective-permute-start.29) | collective-permute-done | bytes 524320 | tf_op jit(solution)/shard_map/ppermute | solution.py:63
  148.8 3.6 collective-permute-done.25.refs_7_
  154.0 12.5 %shard_map.139 = (f32[1600,512]{1,0:T(8,128)}, f32[2,512]{1,0:T(2,128)S(1)}, f32[1600,128]{1,0:T(8,128)S(1)}, bf16[1024,4096]{1,0:T(8,128)(2,1)}, bf16[2048,1024]{1,0:T(8,128)(2,1)}) custom-call(s32[9]{0:T(128)S(1)} %pad_add_fusion.ring_ref, bf16[512,512]{1,0:T(8,128)(2,1)S(1)} %get-tuple-element.32.refs_0_, ...), custom_call_target="tpu_custom_call" | custom-call | flops 6710886400 | bytes 26411008 | tf_op jit(solution)/shard_map/pallas_call | solution.py:234
  167.1 3.2 collective-permute-done.35
  175.8 3.9 %collective-permute-done.37 = f32[2,512]{1,0:T(2,128)S(1)} collective-permute-done((f32[2,512]{1,0:T(2,128)S(1)}, f32[2,512]{1,0:T(2,128)S(1)}, u32[]{:S(2)}, u32[]{:S(2)}) %collective-permute-start.37) | collective-permute-done | bytes 4128 | tf_op jit(solution)/shard_map/ppermute | solution.py:433
  179.8 6.6 %shard_map.140.refs_0_ = bf16[8,1600,128]{2,1,0:T(8,128)(2,1)S(1)} custom-call(s32[8]{0:T(128)S(1)} %select_reduce_fusion.source_ref, s32[8]{0:T(128)S(1)} %convert_element_type.19.present_ref, f32[1600,512]{1,0:T(8,128)} %get-tuple-element.37.gained_ref, bf16[1600,1024]{1,0:T(8,128)(2,1)} %bitcast.28, f32[2,512]{1,0:T(2,128)S(1)} %add_multiply_fusion.2.means_ref.refs_1_, ...), custom_call_target="tpu_custom_call" | custom-call | flops 9830400 | bytes 13107200 | tf_op jit(solution)/shard_map/pallas_call | solution.py:373
  188.1 12.5 %shard_map.142 = (f32[1600,512]{1,0:T(8,128)}, f32[2,512]{1,0:T(2,128)S(1)}, f32[1600,128]{1,0:T(8,128)S(1)}, bf16[1024,4096]{1,0:T(8,128)(2,1)}, bf16[2048,1024]{1,0:T(8,128)(2,1)}) custom-call(s32[9]{0:T(128)S(1)} %pad_add_fusion.ring_ref, bf16[512,512]{1,0:T(8,128)(2,1)S(1)} %get-tuple-element.34.refs_0_, ...), custom_call_target="tpu_custom_call", output_to_operand_aliasing={{3}: (16, {}), {4}: (17, {})} | custom-call | flops 6710886400 | bytes 26411008 | tf_op jit(solution)/shard_map/pallas_call | solution.py:234
  201.5 4.7 %all-to-all-start.1 = ((bf16[8,1600,128]{2,1,0:T(8,128)(2,1)}), bf16[8,1600,128]{2,1,0:T(8,128)(2,1)}, u32[]{:S(2)}, u32[]{:S(2)}) async-start(bf16[8,1600,128]{2,1,0:T(8,128)(2,1)} %copy-done.1), calls=%async_computation.1 | async-start | bytes 6553600 | tf_op jit(solution)/shard_map/all_to_all | solution.py:554
  206.9 5.1 %collective-permute-done.17.b_other_ref = bf16[1024,512]{1,0:T(8,128)(2,1)} collective-permute-done((bf16[1024,512]{1,0:T(8,128)(2,1)}, bf16[1024,512]{1,0:T(8,128)(2,1)}, u32[]{:S(2)}, u32[]{:S(2)}) %collective-permute-start.17) | collective-permute-done | bytes 1048608 | tf_op jit(solution)/shard_map/ppermute | solution.py:425
  213.2 5.1 %shard_map.138.refs_0_ = bf16[1024,512]{1,0:T(8,128)(2,1)S(1)} custom-call(s32[1]{0:T(128)} %bitcast.6.member_ref, bf16[1024,4096]{1,0:T(8,128)(2,1)} %get-tuple-element.28.a_ref, bf16[2048,1024]{1,0:T(8,128)(2,1)} %collective-permute-done.16.a_other_ref, bf16[1024,512]{1,0:T(8,128)(2,1)S(1)} %copy-done.5, bf16[1024,512]{1,0:T(8,128)(2,1)} %collective-permute-done.17.b_other_ref), custom_call_target="tpu_custom_call" | custom-call | flops 2147483648 | bytes 8388608 | tf_op jit(solution)/shard_map/pallas_call | solution.py:297
  218.4 6.6 %shard_map.143.refs_1_ = bf16[800,1024]{1,0:T(8,128)(2,1)S(1)} custom-call(s32[1]{0:T(128)} %bitcast.6.member_ref, bf16[1600,1024]{1,0:T(8,128)(2,1)S(1)} %bitcast.36, bf16[1600,1024]{1,0:T(8,128)(2,1)} %collective-permute-done.38.a_other_ref, bf16[1024,4096]{1,0:T(8,128)(2,1)} %get-tuple-element.41.b_ref, ...), custom_call_target="tpu_custom_call" | custom-call | flops 3355443200 | bytes 10747904 | tf_op jit(solution)/shard_map/pallas_call | solution.py:297
  225.3 3.4 collective-permute-start.44
  228.7 5.1 %collective-permute-done.44 = f32[2,512]{1,0:T(2,128)S(1)} collective-permute-done((f32[2,512]{1,0:T(2,128)S(1)}, f32[2,512]{1,0:T(2,128)S(1)}, u32[]{:S(2)}, u32[]{:S(2)}) %collective-permute-start.44) | collective-permute-done | bytes 4128 | tf_op jit(solution)/shard_map/ppermute | solution.py:433
  235.5 25.9 %collective-permute-done.45 = f32[2,512]{1,0:T(2,128)S(1)} collective-permute-done((f32[2,512]{1,0:T(2,128)S(1)}, f32[2,512]{1,0:T(2,128)S(1)}, u32[]{:S(2)}, u32[]{:S(2)}) %collective-permute-start.45) | collective-permute-done | bytes 4128 | tf_op jit(solution)/shard_map/ppermute | solution.py:433
  261.4 6.3 %shard_map.144.refs_2_ = bf16[800,1024]{1,0:T(8,128)(2,1)S(1)} custom-call(s32[1]{0:T(128)} %bitcast.6.member_ref, bf16[1600,1024]{1,0:T(8,128)(2,1)S(1)} %bitcast.37, bf16[1600,1024]{1,0:T(8,128)(2,1)} %collective-permute-done.38.a_other_ref, bf16[1024,4096]{1,0:T(8,128)(2,1)} %get-tuple-element.41.b_ref, ...), custom_call_target="tpu_custom_call" | custom-call | flops 3355443200 | bytes 10747904 | tf_op jit(solution)/shard_map/pallas_call | solution.py:297
  268.8 3.4 collective-permute-start.46
  272.2 8.6 %collective-permute-done.46 = f32[2,512]{1,0:T(2,128)S(1)} collective-permute-done((f32[2,512]{1,0:T(2,128)S(1)}, f32[2,512]{1,0:T(2,128)S(1)}, u32[]{:S(2)}, u32[]{:S(2)}) %collective-permute-start.46) | collective-permute-done | bytes 4128 | tf_op jit(solution)/shard_map/ppermute | solution.py:433
  280.8 8.3 %shard_map.149.refs_0_ = bf16[8,1600,128]{2,1,0:T(8,128)(2,1)} custom-call(s32[8]{0:T(128)S(1)} %select_reduce_fusion.source_ref, s32[8]{0:T(128)S(1)} %convert_element_type.19.present_ref, f32[1600,512]{1,0:T(8,128)} %get-tuple-element.43.gained_ref, bf16[1600,1024]{1,0:T(8,128)(2,1)} %bitcast.33, f32[2,512]{1,0:T(2,128)S(1)} %add_multiply_fusion.1.means_ref, ...), custom_call_target="tpu_custom_call" | custom-call | flops 9830400 | bytes 13107200 | tf_op jit(solution)/shard_map/pallas_call | solution.py:373
  290.3 3.7 all-to-all-start
  295.5 2.1 collective-permute-start.18
  297.5 2.4 fusion.7
  301.4 5.7 %shard_map.151.refs_0_ = bf16[256,12800]{1,0:T(8,128)(2,1)} custom-call(bf16[12800,128]{1,0:T(8,128)(2,1)} %bitcast.17.in_ref), custom_call_target="tpu_custom_call" | custom-call | bytes 6553600 | tf_op jit(solution)/shard_map/pallas_call | solution.py:410
  307.1 25.9 %collective-permute-done.41.refs_2_.refs_1_ = bf16[800,1024]{1,0:T(8,128)(2,1)} collective-permute-done((bf16[800,1024]{1,0:T(8,128)(2,1)}, bf16[800,1024]{1,0:T(8,128)(2,1)}, u32[]{:S(2)}, u32[]{:S(2)}) %collective-permute-start.41) | collective-permute-done | bytes 1638432 | tf_op jit(solution)/shard_map/ppermute | solution.py:330
  333.1 12.5 %shard_map.147.refs_1_ = f32[1600,1024]{1,0:T(8,128)} custom-call(s32[1]{0:T(128)} %bitcast.member_ref, bf16[1600,1024]{1,0:T(8,128)(2,1)} %bitcast.34, bf16[1600,1024]{1,0:T(8,128)(2,1)} %collective-permute-done.38.a_other_ref, bf16[1024,4096]{1,0:T(8,128)(2,1)} %get-tuple-element.41.b_ref, bf16[2048,1024]{1,0:T(8,128)(2,1)} %collective-permute-done.39.b_other_ref, ...), custom_call_target="tpu_custom_call" | custom-call | flops 6710886400 | bytes 17301504 | tf_op jit(solution)/shard_map/pallas_call | solution.py:297
  345.7 7.8 %collective-permute-done.18.refs_0_ = bf16[1024,512]{1,0:T(8,128)(2,1)} collective-permute-done((bf16[1024,512]{1,0:T(8,128)(2,1)}, bf16[1024,512]{1,0:T(8,128)(2,1)}, u32[]{:S(2)}, u32[]{:S(2)}) %collective-permute-start.18) | collective-permute-done | bytes 1048608 | tf_op jit(solution)/shard_map/ppermute | solution.py:330
  353.5 6.5 %shard_map.146.refs_2_ = f32[1024,512]{1,0:T(8,128)} custom-call(s32[1]{0:T(128)} %bitcast.member_ref, bf16[1024,4096]{1,0:T(8,128)(2,1)} %get-tuple-element.28.a_ref, bf16[2048,1024]{1,0:T(8,128)(2,1)} %collective-permute-done.16.a_other_ref, bf16[1024,512]{1,0:T(8,128)(2,1)S(1)} %copy-done.6, bf16[1024,512]{1,0:T(8,128)(2,1)} %collective-permute-done.17.b_other_ref, ...), custom_call_target="tpu_custom_call" | custom-call | flops 2147483648 | bytes 8388608 | tf_op jit(solution)/shard_map/pallas_call | solution.py:297
  361.2 5.5 %all-to-all-done = bf16[8,1600,128]{2,1,0:T(8,128)(2,1)S(1)} async-done(((bf16[8,1600,128]{2,1,0:T(8,128)(2,1)}), bf16[8,1600,128]{2,1,0:T(8,128)(2,1)S(1)}, u32[]{:S(2)}, u32[]{:S(2)}) %all-to-all-start) | async-done | bytes 3276832 | tf_op jit(solution)/shard_map/all_to_all | solution.py:554
  368.3 3.2 shard_map.152
  (138 shorter events, 52.4 us)
Async XLA Ops:
  1.9 14.9 %collective-permute-start.8 = (bf16[512,512]{1,0:T(8,128)(2,1)S(1)}, bf16[512,512]{1,0:T(8,128)(2,1)S(1)}, u32[]{:S(2)}, u32[]{:S(2)}) collective-permute-start(bf16[512,512]{1,0:T(8,128)(2,1)S(1)} %bitcast.42), channel_id=1, source_target_pairs={{0,2},{2,4},{4,6},{6,7},{7,5},{5,3},{3,1},{1,0},{8,10},{10,12},{12... | collective-permute-start | bytes 1572872 | tf_op jit(solution)/shard_map/ppermute | solution.py:63
  5.0 14.5 %collective-permute-start.9 = (bf16[512,512]{1,0:T(8,128)(2,1)S(1)}, bf16[512,512]{1,0:T(8,128)(2,1)S(1)}, u32[]{:S(2)}, u32[]{:S(2)}) collective-permute-start(bf16[512,512]{1,0:T(8,128)(2,1)S(1)} %bitcast.43), channel_id=1, source_target_pairs={{0,1},{2,0},{4,2},{6,4},{7,6},{5,7},{3,5},{1,3},{8,9},{10,8},{12,1... | collective-permute-start | bytes 1572872 | tf_op jit(solution)/shard_map/ppermute | solution.py:64
  16.9 15.0 %collective-permute-start.10 = (bf16[512,512]{1,0:T(8,128)(2,1)S(1)}, bf16[512,512]{1,0:T(8,128)(2,1)}, u32[]{:S(2)}, u32[]{:S(2)}) collective-permute-start(bf16[512,512]{1,0:T(8,128)(2,1)S(1)} %collective-permute-done.8.refs_1_), channel_id=1, source_target_pairs={{0,2},{2,4},{4,6},{6,7},{7,5},{5,3},{3,1},{1,0},{8,10},{10,12},{12... | collective-permute-start | bytes 1572872 | tf_op jit(solution)/shard_map/ppermute | solution.py:63
  19.5 15.0 %collective-permute-start.11 = (bf16[512,512]{1,0:T(8,128)(2,1)S(1)}, bf16[512,512]{1,0:T(8,128)(2,1)}, u32[]{:S(2)}, u32[]{:S(2)}) collective-permute-start(bf16[512,512]{1,0:T(8,128)(2,1)S(1)} %collective-permute-done.9.refs_2_), channel_id=1, source_target_pairs={{0,1},{2,0},{4,2},{6,4},{7,6},{5,7},{3,5},{1,3},{8,9},{10,8},{12,1... | collective-permute-start | bytes 1572872 | tf_op jit(solution)/shard_map/ppermute | solution.py:64
  20.5 22.5 %collective-permute-start = (bf16[512,512]{1,0:T(8,128)(2,1)S(1)}, bf16[512,512]{1,0:T(8,128)(2,1)S(1)}, u32[]{:S(2)}, u32[]{:S(2)}) collective-permute-start(bf16[512,512]{1,0:T(8,128)(2,1)S(1)} %bitcast.39), channel_id=1, source_target_pairs={{0,2},{2,4},{4,6},{6,7},{7,5},{5,3},{3,1},{1,0},{8,10},{10,12},{12... | collective-permute-start | bytes 1572872 | tf_op jit(solution)/shard_map/ppermute | solution.py:63
  22.3 23.3 %collective-permute-start.1 = (bf16[512,512]{1,0:T(8,128)(2,1)S(1)}, bf16[512,512]{1,0:T(8,128)(2,1)S(1)}, u32[]{:S(2)}, u32[]{:S(2)}) collective-permute-start(bf16[512,512]{1,0:T(8,128)(2,1)S(1)} %bitcast.40), channel_id=1, source_target_pairs={{0,1},{2,0},{4,2},{6,4},{7,6},{5,7},{3,5},{1,3},{8,9},{10,8},{12,1... | collective-permute-start | bytes 1572872 | tf_op jit(solution)/shard_map/ppermute | solution.py:64
  31.9 22.4 %collective-permute-start.12 = (bf16[512,512]{1,0:T(8,128)(2,1)}, bf16[512,512]{1,0:T(8,128)(2,1)S(1)}, u32[]{:S(2)}, u32[]{:S(2)}) collective-permute-start(bf16[512,512]{1,0:T(8,128)(2,1)} %collective-permute-done.10.refs_3_), channel_id=1, source_target_pairs={{0,2},{2,4},{4,6},{6,7},{7,5},{5,3},{3,1},{1,0},{8,10},{10,12},{12... | collective-permute-start | bytes 1572872 | tf_op jit(solution)/shard_map/ppermute | solution.py:63
  34.4 22.4 %collective-permute-start.13 = (bf16[512,512]{1,0:T(8,128)(2,1)}, bf16[512,512]{1,0:T(8,128)(2,1)S(1)}, u32[]{:S(2)}, u32[]{:S(2)}) collective-permute-start(bf16[512,512]{1,0:T(8,128)(2,1)} %collective-permute-done.11.refs_4_), channel_id=1, source_target_pairs={{0,1},{2,0},{4,2},{6,4},{7,6},{5,7},{3,5},{1,3},{8,9},{10,8},{12,1... | collective-permute-start | bytes 1572872 | tf_op jit(solution)/shard_map/ppermute | solution.py:64
  43.0 22.5 %collective-permute-start.2 = (bf16[512,512]{1,0:T(8,128)(2,1)S(1)}, bf16[512,512]{1,0:T(8,128)(2,1)S(1)}, u32[]{:S(2)}, u32[]{:S(2)}) collective-permute-start(bf16[512,512]{1,0:T(8,128)(2,1)S(1)} %collective-permute-done.refs_1_), channel_id=1, source_target_pairs={{0,2},{2,4},{4,6},{6,7},{7,5},{5,3},{3,1},{1,0},{8,10},{10,12},{12... | collective-permute-start | bytes 1572872 | tf_op jit(solution)/shard_map/ppermute | solution.py:63
  45.6 22.5 %collective-permute-start.3 = (bf16[512,512]{1,0:T(8,128)(2,1)S(1)}, bf16[512,512]{1,0:T(8,128)(2,1)S(1)}, u32[]{:S(2)}, u32[]{:S(2)}) collective-permute-start(bf16[512,512]{1,0:T(8,128)(2,1)S(1)} %collective-permute-done.1.refs_2_), channel_id=1, source_target_pairs={{0,1},{2,0},{4,2},{6,4},{7,6},{5,7},{3,5},{1,3},{8,9},{10,8},{12,1... | collective-permute-start | bytes 1572872 | tf_op jit(solution)/shard_map/ppermute | solution.py:64
  54.2 16.8 %collective-permute-start.14 = (bf16[256,512]{1,0:T(8,128)(2,1)S(1)}, bf16[256,512]{1,0:T(8,128)(2,1)S(1)}, u32[]{:S(2)}, u32[]{:S(2)}) collective-permute-start(bf16[256,512]{1,0:T(8,128)(2,1)S(1)} %slice.60), channel_id=1, source_target_pairs={{0,2},{2,4},{4,6},{6,7},{7,5},{5,3},{3,1},{1,0},{8,10},{10,12},{12... | collective-permute-start | bytes 786440 | tf_op jit(solution)/shard_map/ppermute | solution.py:67
  56.8 16.8 %collective-permute-start.15 = (bf16[256,512]{1,0:T(8,128)(2,1)S(1)}, bf16[256,512]{1,0:T(8,128)(2,1)S(1)}, u32[]{:S(2)}, u32[]{:S(2)}) collective-permute-start(bf16[256,512]{1,0:T(8,128)(2,1)S(1)} %slice.61), channel_id=1, source_target_pairs={{0,1},{2,0},{4,2},{6,4},{7,6},{5,7},{3,5},{1,3},{8,9},{10,8},{12,1... | collective-permute-start | bytes 786440 | tf_op jit(solution)/shard_map/ppermute | solution.py:68
  65.5 17.5 %collective-permute-start.4 = (bf16[512,512]{1,0:T(8,128)(2,1)S(1)}, bf16[512,512]{1,0:T(8,128)(2,1)S(1)}, u32[]{:S(2)}, u32[]{:S(2)}) collective-permute-start(bf16[512,512]{1,0:T(8,128)(2,1)S(1)} %collective-permute-done.2.refs_3_), channel_id=1, source_target_pairs={{0,2},{2,4},{4,6},{6,7},{7,5},{5,3},{3,1},{1,0},{8,10},{10,12},{12... | collective-permute-start | bytes 1572872 | tf_op jit(solution)/shard_map/ppermute | solution.py:63
  68.1 16.7 %collective-permute-start.5 = (bf16[512,512]{1,0:T(8,128)(2,1)S(1)}, bf16[512,512]{1,0:T(8,128)(2,1)S(1)}, u32[]{:S(2)}, u32[]{:S(2)}) collective-permute-start(bf16[512,512]{1,0:T(8,128)(2,1)S(1)} %collective-permute-done.3.refs_4_), channel_id=1, source_target_pairs={{0,1},{2,0},{4,2},{6,4},{7,6},{5,7},{3,5},{1,3},{8,9},{10,8},{12,1... | collective-permute-start | bytes 1572872 | tf_op jit(solution)/shard_map/ppermute | solution.py:64
  80.9 14.9 %collective-permute-start.19 = (bf16[512,512]{1,0:T(8,128)(2,1)S(1)}, bf16[512,512]{1,0:T(8,128)(2,1)S(1)}, u32[]{:S(2)}, u32[]{:S(2)}) collective-permute-start(bf16[512,512]{1,0:T(8,128)(2,1)S(1)} %get-tuple-element.32.refs_0_), channel_id=1, source_target_pairs={{0,2},{2,4},{4,6},{6,7},{7,5},{5,3},{3,1},{1,0},{8,10},{10,12},{12... | collective-permute-start | bytes 1572872 | tf_op jit(solution)/shard_map/ppermute | solution.py:63
  82.5 14.9 %collective-permute-start.20 = (bf16[512,512]{1,0:T(8,128)(2,1)S(1)}, bf16[512,512]{1,0:T(8,128)(2,1)S(1)}, u32[]{:S(2)}, u32[]{:S(2)}) collective-permute-start(bf16[512,512]{1,0:T(8,128)(2,1)S(1)} %get-tuple-element.32.refs_0_), channel_id=1, source_target_pairs={{0,1},{2,0},{4,2},{6,4},{7,6},{5,7},{3,5},{1,3},{8,9},{10,8},{12,1... | collective-permute-start | bytes 1572872 | tf_op jit(solution)/shard_map/ppermute | solution.py:64
  83.0 18.4 %collective-permute-start.6 = (bf16[256,512]{1,0:T(8,128)(2,1)S(1)}, bf16[256,512]{1,0:T(8,128)(2,1)S(1)}, u32[]{:S(2)}, u32[]{:S(2)}) collective-permute-start(bf16[256,512]{1,0:T(8,128)(2,1)S(1)} %slice.57), channel_id=1, source_target_pairs={{0,2},{2,4},{4,6},{6,7},{7,5},{5,3},{3,1},{1,0},{8,10},{10,12},{12... | collective-permute-start | bytes 786440 | tf_op jit(solution)/shard_map/ppermute | solution.py:67
  84.8 18.2 %collective-permute-start.7 = (bf16[256,512]{1,0:T(8,128)(2,1)S(1)}, bf16[256,512]{1,0:T(8,128)(2,1)S(1)}, u32[]{:S(2)}, u32[]{:S(2)}) collective-permute-start(bf16[256,512]{1,0:T(8,128)(2,1)S(1)} %slice.58), channel_id=1, source_target_pairs={{0,1},{2,0},{4,2},{6,4},{7,6},{5,7},{3,5},{1,3},{8,9},{10,8},{12,1... | collective-permute-start | bytes 786440 | tf_op jit(solution)/shard_map/ppermute | solution.py:68
  95.8 16.5 %collective-permute-start.21 = (bf16[512,512]{1,0:T(8,128)(2,1)S(1)}, bf16[512,512]{1,0:T(8,128)(2,1)S(1)}, u32[]{:S(2)}, u32[]{:S(2)}) collective-permute-start(bf16[512,512]{1,0:T(8,128)(2,1)S(1)} %collective-permute-done.19.refs_1_), channel_id=1, source_target_pairs={{0,2},{2,4},{4,6},{6,7},{7,5},{5,3},{3,1},{1,0},{8,10},{10,12},{12... | collective-permute-start | bytes 1572872 | tf_op jit(solution)/shard_map/ppermute | solution.py:63
  97.4 16.9 %collective-permute-start.22 = (bf16[512,512]{1,0:T(8,128)(2,1)S(1)}, bf16[512,512]{1,0:T(8,128)(2,1)S(1)}, u32[]{:S(2)}, u32[]{:S(2)}) collective-permute-start(bf16[512,512]{1,0:T(8,128)(2,1)S(1)} %collective-permute-done.20.refs_2_), channel_id=1, source_target_pairs={{0,1},{2,0},{4,2},{6,4},{7,6},{5,7},{3,5},{1,3},{8,9},{10,8},{12,1... | collective-permute-start | bytes 1572872 | tf_op jit(solution)/shard_map/ppermute | solution.py:64
  109.4 14.9 %collective-permute-start.27 = (bf16[512,512]{1,0:T(8,128)(2,1)S(1)}, bf16[512,512]{1,0:T(8,128)(2,1)S(1)}, u32[]{:S(2)}, u32[]{:S(2)}) collective-permute-start(bf16[512,512]{1,0:T(8,128)(2,1)S(1)} %get-tuple-element.34.refs_0_), channel_id=1, source_target_pairs={{0,2},{2,4},{4,6},{6,7},{7,5},{5,3},{3,1},{1,0},{8,10},{10,12},{12... | collective-permute-start | bytes 1572872 | tf_op jit(solution)/shard_map/ppermute | solution.py:63
  111.0 14.9 %collective-permute-start.28 = (bf16[512,512]{1,0:T(8,128)(2,1)S(1)}, bf16[512,512]{1,0:T(8,128)(2,1)S(1)}, u32[]{:S(2)}, u32[]{:S(2)}) collective-permute-start(bf16[512,512]{1,0:T(8,128)(2,1)S(1)} %get-tuple-element.34.refs_0_), channel_id=1, source_target_pairs={{0,1},{2,0},{4,2},{6,4},{7,6},{5,7},{3,5},{1,3},{8,9},{10,8},{12,1... | collective-permute-start | bytes 1572872 | tf_op jit(solution)/shard_map/ppermute | solution.py:64
  112.3 23.3 %collective-permute-start.23 = (bf16[512,512]{1,0:T(8,128)(2,1)S(1)}, bf16[512,512]{1,0:T(8,128)(2,1)S(1)}, u32[]{:S(2)}, u32[]{:S(2)}) collective-permute-start(bf16[512,512]{1,0:T(8,128)(2,1)S(1)} %collective-permute-done.21.refs_3_), channel_id=1, source_target_pairs={{0,2},{2,4},{4,6},{6,7},{7,5},{5,3},{3,1},{1,0},{8,10},{10,12},{12... | collective-permute-start | bytes 1572872 | tf_op jit(solution)/shard_map/ppermute | solution.py:63
  114.2 23.0 %collective-permute-start.24 = (bf16[512,512]{1,0:T(8,128)(2,1)S(1)}, bf16[512,512]{1,0:T(8,128)(2,1)S(1)}, u32[]{:S(2)}, u32[]{:S(2)}) collective-permute-start(bf16[512,512]{1,0:T(8,128)(2,1)S(1)} %collective-permute-done.22.refs_4_), channel_id=1, source_target_pairs={{0,1},{2,0},{4,2},{6,4},{7,6},{5,7},{3,5},{1,3},{8,9},{10,8},{12,1... | collective-permute-start | bytes 1572872 | tf_op jit(solution)/shard_map/ppermute | solution.py:64
  124.3 22.5 %collective-permute-start.29 = (bf16[512,512]{1,0:T(8,128)(2,1)S(1)}, bf16[512,512]{1,0:T(8,128)(2,1)S(1)}, u32[]{:S(2)}, u32[]{:S(2)}) collective-permute-start(bf16[512,512]{1,0:T(8,128)(2,1)S(1)} %collective-permute-done.27.refs_1_), channel_id=1, source_target_pairs={{0,2},{2,4},{4,6},{6,7},{7,5},{5,3},{3,1},{1,0},{8,10},{10,12},{12... | collective-permute-start | bytes 1572872 | tf_op jit(solution)/shard_map/ppermute | solution.py:63
  125.9 22.5 %collective-permute-start.30 = (bf16[512,512]{1,0:T(8,128)(2,1)S(1)}, bf16[512,512]{1,0:T(8,128)(2,1)S(1)}, u32[]{:S(2)}, u32[]{:S(2)}) collective-permute-start(bf16[512,512]{1,0:T(8,128)(2,1)S(1)} %collective-permute-done.28.refs_2_), channel_id=1, source_target_pairs={{0,1},{2,0},{4,2},{6,4},{7,6},{5,7},{3,5},{1,3},{8,9},{10,8},{12,1... | collective-permute-start | bytes 1572872 | tf_op jit(solution)/shard_map/ppermute | solution.py:64
  135.6 16.8 %collective-permute-start.25 = (bf16[256,512]{1,0:T(8,128)(2,1)S(1)}, bf16[256,512]{1,0:T(8,128)(2,1)S(1)}, u32[]{:S(2)}, u32[]{:S(2)}) collective-permute-start(bf16[256,512]{1,0:T(8,128)(2,1)S(1)} %slice.62), channel_id=1, source_target_pairs={{0,2},{2,4},{4,6},{6,7},{7,5},{5,3},{3,1},{1,0},{8,10},{10,12},{12... | collective-permute-start | bytes 786440 | tf_op jit(solution)/shard_map/ppermute | solution.py:67
  137.2 16.7 %collective-permute-start.26 = (bf16[256,512]{1,0:T(8,128)(2,1)S(1)}, bf16[256,512]{1,0:T(8,128)(2,1)S(1)}, u32[]{:S(2)}, u32[]{:S(2)}) collective-permute-start(bf16[256,512]{1,0:T(8,128)(2,1)S(1)} %slice.63), channel_id=1, source_target_pairs={{0,1},{2,0},{4,2},{6,4},{7,6},{5,7},{3,5},{1,3},{8,9},{10,8},{12,1... | collective-permute-start | bytes 786440 | tf_op jit(solution)/shard_map/ppermute | solution.py:68
  146.8 25.1 %collective-permute-start.31 = (bf16[512,512]{1,0:T(8,128)(2,1)S(1)}, bf16[512,512]{1,0:T(8,128)(2,1)S(1)}, u32[]{:S(2)}, u32[]{:S(2)}) collective-permute-start(bf16[512,512]{1,0:T(8,128)(2,1)S(1)} %collective-permute-done.29.refs_3_), channel_id=1, source_target_pairs={{0,2},{2,4},{4,6},{6,7},{7,5},{5,3},{3,1},{1,0},{8,10},{10,12},{12... | collective-permute-start | bytes 1572872 | tf_op jit(solution)/shard_map/ppermute | solution.py:63
  148.4 24.0 %collective-permute-start.32 = (bf16[512,512]{1,0:T(8,128)(2,1)S(1)}, bf16[512,512]{1,0:T(8,128)(2,1)S(1)}, u32[]{:S(2)}, u32[]{:S(2)}) collective-permute-start(bf16[512,512]{1,0:T(8,128)(2,1)S(1)} %collective-permute-done.30.refs_4_), channel_id=1, source_target_pairs={{0,1},{2,0},{4,2},{6,4},{7,6},{5,7},{3,5},{1,3},{8,9},{10,8},{12,1... | collective-permute-start | bytes 1572872 | tf_op jit(solution)/shard_map/ppermute | solution.py:64
  170.2 4.0 %collective-permute-start.36 = (f32[2,512]{1,0:T(2,128)S(1)}, f32[2,512]{1,0:T(2,128)S(1)}, u32[]{:S(2)}, u32[]{:S(2)}) collective-permute-start(f32[2,512]{1,0:T(2,128)S(1)} %add.73), channel_id=1, source_target_pairs={{0,2},{1,3},{2,0},{3,1},{4,6},{5,7},{6,4},{7,5},{8,10},{9,11},{10,... | collective-permute-start | bytes 12296 | tf_op jit(solution)/shard_map/ppermute | solution.py:433
  171.9 14.5 %collective-permute-start.33 = (bf16[256,512]{1,0:T(8,128)(2,1)S(1)}, bf16[256,512]{1,0:T(8,128)(2,1)S(1)}, u32[]{:S(2)}, u32[]{:S(2)}) collective-permute-start(bf16[256,512]{1,0:T(8,128)(2,1)S(1)} %slice.64), channel_id=1, source_target_pairs={{0,2},{2,4},{4,6},{6,7},{7,5},{5,3},{3,1},{1,0},{8,10},{10,12},{12... | collective-permute-start | bytes 786440 | tf_op jit(solution)/shard_map/ppermute | solution.py:67
  172.5 13.9 %collective-permute-start.34 = (bf16[256,512]{1,0:T(8,128)(2,1)S(1)}, bf16[256,512]{1,0:T(8,128)(2,1)S(1)}, u32[]{:S(2)}, u32[]{:S(2)}) collective-permute-start(bf16[256,512]{1,0:T(8,128)(2,1)S(1)} %slice.65), channel_id=1, source_target_pairs={{0,1},{2,0},{4,2},{6,4},{7,6},{5,7},{3,5},{1,3},{8,9},{10,8},{12,1... | collective-permute-start | bytes 786440 | tf_op jit(solution)/shard_map/ppermute | solution.py:68
  174.2 5.5 %collective-permute-start.37 = (f32[2,512]{1,0:T(2,128)S(1)}, f32[2,512]{1,0:T(2,128)S(1)}, u32[]{:S(2)}, u32[]{:S(2)}) collective-permute-start(f32[2,512]{1,0:T(2,128)S(1)} %add.74), channel_id=1, source_target_pairs={{0,4},{1,5},{2,6},{3,7},{4,0},{5,1},{6,2},{7,3},{8,12},{9,13},{10,... | collective-permute-start | bytes 12296 | tf_op jit(solution)/shard_map/ppermute | solution.py:433
  175.7 36.2 %collective-permute-start.16 = (bf16[2048,1024]{1,0:T(8,128)(2,1)}, bf16[2048,1024]{1,0:T(8,128)(2,1)}, u32[]{:S(2)}, u32[]{:S(2)}) collective-permute-start(bf16[2048,1024]{1,0:T(8,128)(2,1)} %get-tuple-element.29), channel_id=1, source_target_pairs={{0,8},{8,0},{16,24},{24,16},{1,9},{9,1},{17,25},{25,17},{2,10},{10... | collective-permute-start | bytes 12582920 | tf_op jit(solution)/shard_map/ppermute | solution.py:425
  201.5 16.9 %collective-permute-start.39 = (bf16[2048,1024]{1,0:T(8,128)(2,1)}, bf16[2048,1024]{1,0:T(8,128)(2,1)}, u32[]{:S(2)}, u32[]{:S(2)}) collective-permute-start(bf16[2048,1024]{1,0:T(8,128)(2,1)} %get-tuple-element.42), channel_id=1, source_target_pairs={{0,8},{8,0},{16,24},{24,16},{1,9},{9,1},{17,25},{25,17},{2,10},{10... | collective-permute-start | bytes 12582920 | tf_op jit(solution)/shard_map/ppermute | solution.py:425
  201.5 88.8 %all-to-all-start.1 = ((bf16[8,1600,128]{2,1,0:T(8,128)(2,1)}), bf16[8,1600,128]{2,1,0:T(8,128)(2,1)}, u32[]{:S(2)}, u32[]{:S(2)}) async-start(bf16[8,1600,128]{2,1,0:T(8,128)(2,1)} %copy-done.1), calls=%async_computation.1 | async-start | bytes 6553600 | tf_op jit(solution)/shard_map/all_to_all | solution.py:554
  206.2 12.1 %collective-permute-start.38 = (bf16[1600,1024]{1,0:T(8,128)(2,1)S(1)}, bf16[1600,1024]{1,0:T(8,128)(2,1)}, u32[]{:S(2)}, u32[]{:S(2)}) collective-permute-start(bf16[1600,1024]{1,0:T(8,128)(2,1)S(1)} %bitcast.35), channel_id=1, source_target_pairs={{0,8},{8,0},{16,24},{24,16},{1,9},{9,1},{17,25},{25,17},{2,10},{10... | collective-permute-start | bytes 9830408 | tf_op jit(solution)/shard_map/ppermute | solution.py:425
  206.8 5.2 %collective-permute-start.17 = (bf16[1024,512]{1,0:T(8,128)(2,1)}, bf16[1024,512]{1,0:T(8,128)(2,1)}, u32[]{:S(2)}, u32[]{:S(2)}) collective-permute-start(bf16[1024,512]{1,0:T(8,128)(2,1)} %get-tuple-element.46.b_ref), channel_id=1, source_target_pairs={{0,8},{8,0},{16,24},{24,16},{1,9},{9,1},{17,25},{25,17},{2,10},{10... | collective-permute-start | bytes 3145736 | tf_op jit(solution)/shard_map/ppermute | solution.py:425
  225.0 64.1 %collective-permute-start.40 = (bf16[800,1024]{1,0:T(8,128)(2,1)S(1)}, bf16[800,1024]{1,0:T(8,128)(2,1)S(1)}, u32[]{:S(2)}, u32[]{:S(2)}) collective-permute-start(bf16[800,1024]{1,0:T(8,128)(2,1)S(1)} %shard_map.143.refs_1_), channel_id=1, source_target_pairs={{0,16},{8,24},{16,0},{24,8},{1,17},{9,25},{17,1},{25,9},{2,18},{10... | collective-permute-start | bytes 4915208 | tf_op jit(solution)/shard_map/ppermute | solution.py:330
  225.3 8.5 %collective-permute-start.44 = (f32[2,512]{1,0:T(2,128)S(1)}, f32[2,512]{1,0:T(2,128)S(1)}, u32[]{:S(2)}, u32[]{:S(2)}) collective-permute-start(f32[2,512]{1,0:T(2,128)S(1)} %get-tuple-element.44), channel_id=1, source_target_pairs={{0,1},{1,0},{2,3},{3,2},{4,5},{5,4},{6,7},{7,6},{8,9},{9,8},{10,11... | collective-permute-start | bytes 12296 | tf_op jit(solution)/shard_map/ppermute | solution.py:433
  233.8 27.5 %collective-permute-start.45 = (f32[2,512]{1,0:T(2,128)S(1)}, f32[2,512]{1,0:T(2,128)S(1)}, u32[]{:S(2)}, u32[]{:S(2)}) collective-permute-start(f32[2,512]{1,0:T(2,128)S(1)} %add.79), channel_id=1, source_target_pairs={{0,2},{1,3},{2,0},{3,1},{4,6},{5,7},{6,4},{7,5},{8,10},{9,11},{10,... | collective-permute-start | bytes 12296 | tf_op jit(solution)/shard_map/ppermute | solution.py:433
  268.8 12.0 %collective-permute-start.46 = (f32[2,512]{1,0:T(2,128)S(1)}, f32[2,512]{1,0:T(2,128)S(1)}, u32[]{:S(2)}, u32[]{:S(2)}) collective-permute-start(f32[2,512]{1,0:T(2,128)S(1)} %shard_map.148), channel_id=1, source_target_pairs={{0,4},{1,5},{2,6},{3,7},{4,0},{5,1},{6,2},{7,3},{8,12},{9,13},{10,... | collective-permute-start | bytes 12296 | tf_op jit(solution)/shard_map/ppermute | solution.py:433
  290.3 76.4 %all-to-all-start = ((bf16[8,1600,128]{2,1,0:T(8,128)(2,1)}), bf16[8,1600,128]{2,1,0:T(8,128)(2,1)S(1)}, u32[]{:S(2)}, u32[]{:S(2)}) async-start(bf16[8,1600,128]{2,1,0:T(8,128)(2,1)} %shard_map.150), calls=%async_computation | async-start | bytes 6553600 | tf_op jit(solution)/shard_map/all_to_all | solution.py:554
  293.9 39.1 %collective-permute-start.41 = (bf16[800,1024]{1,0:T(8,128)(2,1)}, bf16[800,1024]{1,0:T(8,128)(2,1)}, u32[]{:S(2)}, u32[]{:S(2)}) collective-permute-start(bf16[800,1024]{1,0:T(8,128)(2,1)} %copy-done.8), channel_id=1, source_target_pairs={{0,16},{8,24},{16,0},{24,8},{1,17},{9,25},{17,1},{25,9},{2,18},{10... | collective-permute-start | bytes 4915208 | tf_op jit(solution)/shard_map/ppermute | solution.py:330
  295.5 58.0 %collective-permute-start.18 = (bf16[1024,512]{1,0:T(8,128)(2,1)}, bf16[1024,512]{1,0:T(8,128)(2,1)}, u32[]{:S(2)}, u32[]{:S(2)}) collective-permute-start(bf16[1024,512]{1,0:T(8,128)(2,1)} %copy-done.4), channel_id=1, source_target_pairs={{0,16},{8,24},{16,0},{24,8},{1,17},{9,25},{17,1},{25,9},{2,18},{10... | collective-permute-start | bytes 3145736 | tf_op jit(solution)/shard_map/ppermute | solution.py:330
  333.1 12.5 %collective-permute-start.42 = (f32[4224]{0:T(1024)S(1)}, f32[4224]{0:T(1024)S(1)}, u32[]{:S(2)}, u32[]{:S(2)}) collective-permute-start(f32[4224]{0:T(1024)S(1)} %shard_map.145.refs_1_), channel_id=1, source_target_pairs={{0,8},{8,0},{16,24},{24,16},{1,9},{9,1},{17,25},{25,17},{2,10},{10... | collective-permute-start | bytes 50696 | tf_op jit(solution)/shard_map/ppermute | solution.py:433
  345.6 14.3 %collective-permute-start.43 = (f32[4224]{0:T(1024)S(1)}, f32[4224]{0:T(1024)S(1)}, u32[]{:S(2)}, u32[]{:S(2)}) collective-permute-start(f32[4224]{0:T(1024)S(1)} %add.77), channel_id=1, source_target_pairs={{0,16},{8,24},{16,0},{24,8},{1,17},{9,25},{17,1},{25,9},{2,18},{10... | collective-permute-start | bytes 50696 | tf_op jit(solution)/shard_map/ppermute | solution.py:433
  (19 other events, 299.5 us)
where the time goes:
time: 373 us; the launch traced here: 371 us
  waiting for transfers between devices  192 us (51%)
  Pallas kernels  99.4 us (27%)
  starting transfers between devices  57.4 us (15%)
  local copies, waits for them, and re-layouts  14.5 us (4%)
  other arithmetic  7.46 us (2%)
    ppermute x12, waiting for transfers between devices, ring_blocks(): up = lax.ppermute(up, 'tp', ahead)  81.1 us
    ppermute x8, waiting for transfers between devices, doubling_sum(): lax.ppermute(value, axis, [(t, t ^ bit) for t in range(count)])  46.8 us
    pallas_call x5, Pallas kernels, pair_product(): pl.pallas_call(functools.partial(pair_kernel, contract, scale, [span for...  37 us
    ppermute x3, waiting for transfers between devices, chip_products(): arrived.append((span, lax.ppermute(going[-1], 'ctx', route)))  33.7 us
    pallas_call x2, Pallas kernels, norm_part(): pl.pallas_call(functools.partial(norm_kernel, chunk, image_rows, len(bloc...  25 us
    ppermute x12, starting transfers between devices, ring_blocks(): up = lax.ppermute(up, 'tp', ahead)  21.4 us
    pallas_call x2, Pallas kernels, visual_slots(): pl.pallas_call(visual_kernel, grid_spec=pltpu.PrefetchScalarGridSpec(num_...  14.8 us
    pallas_call x2, Pallas kernels, back_part(): pl.pallas_call(functools.partial(back_kernel, chunk, image_rows, len(bloc...  13.6 us
  transfers between devices with their start and end apart: 49, of which 31 were waited for; matrix products, arithmetic and copies ran while one was open for 3% of the time, Pallas kernels for 26%

commit v1 on v0

--- a/solution.py
+++ b/solution.py
@@ -335,11 +335,12 @@
     del refs
 
 
-def tie(values, others):
+def tie(values, others, place=pl.ANY):
+    spaces = [place] + [pl.ANY] * (len(values) + len(others) - 1)
     return pl.pallas_call(
         tie_kernel,
-        in_specs=[pl.BlockSpec(memory_space=pl.ANY)] * (len(values) + len(others)),
-        out_specs=[pl.BlockSpec(memory_space=pl.ANY)] * len(values),
+        in_specs=[pl.BlockSpec(memory_space=space) for space in spaces],
+        out_specs=[pl.BlockSpec(memory_space=space) for space in spaces[: len(values)]],
         out_shape=[jax.ShapeDtypeStruct(value.shape, value.dtype) for value in values],
         input_output_aliases={n: n for n in range(len(values))},
         compiler_params=pltpu.CompilerParams(vmem_limit_bytes=VMEM_LIMIT),
@@ -517,7 +518,7 @@
     first_gained, first_rows, first_ln, *so_far = norm_of(0, first_backs, (), [])
     first_means = doubling_sum(first_rows, "tp", tp_count) / full_width
     first_slots, first_means = tie(
-        [slots_of(0, first_gained, first_means), first_means], second_backs[-2:]
+        [slots_of(0, first_gained, first_means), first_means], second_backs[-2:], pltpu.HBM
     )
     outgoing = [first_slots]
     second_gained, second_rows, second_ln, backs, backs_swap = norm_of(
@@ -545,11 +546,11 @@
 
     cut = w1_tiles // 2
     spans = [(0, cut), (cut, w1_tiles)] if cut else [(0, w1_tiles)]
-    going_w1, arrived_w1 = chip_products(grad_w1_share, spans, ctx_count, going_w2)
+    going_w1, arrived_w1 = chip_products(grad_w1_share, spans, ctx_count, [])
 
     second_means = doubling_sum(second_rows, "tp", tp_count, going_w1) / full_width
     early = [part for span, part in arrived_w1 if span == spans[0]]
-    outgoing += tie([slots_of(1, second_gained, second_means)], early)
+    outgoing += tie([slots_of(1, second_gained, second_means)], early, pltpu.HBM)
     received = [
         lax.all_to_all(part, "tp", split_axis=0, concat_axis=0, tiled=True) for part in outgoing
     ]

time: 373 us -> 371 us (level)
    ppermute x8, waiting for transfers between devices: 46.8 us -> 54.1 us  [doubling_sum(): lax.ppermute(value, axis, [(t, t ^ bit) for t in range(count)])]
    ppermute x3, waiting for transfers between devices: 33.7 us -> 28.1 us  [chip_products(): arrived.append((span, lax.ppermute(going[-1], 'ctx', route)))]
    unnamed x36 -> x42, local copies, waits for them, and re-layouts: 9.36 us -> 9.65 us
  transfers between devices with their start and end apart: 49 -> 49, of which waited for: 31 -> 32; matrix products, arithmetic and copies ran while one was open for 3% -> 3% of each run, Pallas kernels for 26% -> 22%
where the time goes in v1:
time: 371 us
  waiting for transfers between devices  195 us (53%)
  Pallas kernels  97.5 us (26%)
  starting transfers between devices  56.3 us (15%)
  local copies, waits for them, and re-layouts  14.8 us (4%)
  other arithmetic  6.06 us (2%)
    ppermute x12, waiting for transfers between devices, ring_blocks(): up = lax.ppermute(up, 'tp', ahead)  81.1 us
    ppermute x8, waiting for transfers between devices, doubling_sum(): lax.ppermute(value, axis, [(t, t ^ bit) for t in range(count)])  54.1 us
    pallas_call x5, Pallas kernels, pair_product(): pl.pallas_call(functools.partial(pair_kernel, contract, scale, [span for...  36.8 us
    ppermute x3, waiting for transfers between devices, chip_products(): arrived.append((span, lax.ppermute(going[-1], 'ctx', route)))  28.1 us
    pallas_call x2, Pallas kernels, norm_part(): pl.pallas_call(functools.partial(norm_kernel, chunk, image_rows, len(bloc...  25 us
    ppermute x12, starting transfers between devices, ring_blocks(): up = lax.ppermute(up, 'tp', ahead)  21.4 us
    pallas_call x2, Pallas kernels, back_part(): pl.pallas_call(functools.partial(back_kernel, chunk, image_rows, len(bloc...  13.5 us
    pallas_call x2, Pallas kernels, visual_slots(): pl.pallas_call(visual_kernel, grid_spec=pltpu.PrefetchScalarGridSpec(num_...  13.4 us
  transfers between devices with their start and end apart: 49, of which 32 were waited for; matrix products, arithmetic and copies ran while one was open for 3% of the time, Pallas kernels for 22%

profile of v1, /device:TPU:0, one launch (start us, length us, event | category | flops | bytes accessed | tf_op | source)
XLA Modules:
  0.0 370.7 jit_solution(16525381050517915434)
XLA Ops:
  1.9 3.1 collective-permute-start.8
  5.0 11.9 %collective-permute-done.8.refs_1_ = bf16[512,512]{1,0:T(8,128)(2,1)S(1)} collective-permute-done((bf16[512,512]{1,0:T(8,128)(2,1)S(1)}, bf16[512,512]{1,0:T(8,128)(2,1)S(1)}, u32[]{:S(2)}, u32[]{:S(2)}) %collective-permute-start.8) | collective-permute-done | bytes 524320 | tf_op jit(solution)/shard_map/ppermute | solution.py:63
  16.9 1.8 collective-permute-start.10
  20.5 1.8 collective-permute-start
  22.5 9.3 %collective-permute-done.10.refs_3_ = bf16[512,512]{1,0:T(8,128)(2,1)} collective-permute-done((bf16[512,512]{1,0:T(8,128)(2,1)S(1)}, bf16[512,512]{1,0:T(8,128)(2,1)}, u32[]{:S(2)}, u32[]{:S(2)}) %collective-permute-start.10) | collective-permute-done | bytes 524320 | tf_op jit(solution)/shard_map/ppermute | solution.py:63
  31.9 1.8 collective-permute-start.12
  34.7 8.3 %collective-permute-done.refs_1_ = bf16[512,512]{1,0:T(8,128)(2,1)S(1)} collective-permute-done((bf16[512,512]{1,0:T(8,128)(2,1)S(1)}, bf16[512,512]{1,0:T(8,128)(2,1)S(1)}, u32[]{:S(2)}, u32[]{:S(2)}) %collective-permute-start) | collective-permute-done | bytes 524320 | tf_op jit(solution)/shard_map/ppermute | solution.py:63
  43.0 1.8 collective-permute-start.2
  46.6 7.6 %collective-permute-done.12.refs_5_ = bf16[512,512]{1,0:T(8,128)(2,1)S(1)} collective-permute-done((bf16[512,512]{1,0:T(8,128)(2,1)}, bf16[512,512]{1,0:T(8,128)(2,1)S(1)}, u32[]{:S(2)}, u32[]{:S(2)}) %collective-permute-start.12) | collective-permute-done | bytes 524320 | tf_op jit(solution)/shard_map/ppermute | solution.py:63
  54.2 1.8 collective-permute-start.14
  57.1 3.2 fusion.6
  60.3 5.2 %collective-permute-done.2.refs_3_ = bf16[512,512]{1,0:T(8,128)(2,1)S(1)} collective-permute-done((bf16[512,512]{1,0:T(8,128)(2,1)S(1)}, bf16[512,512]{1,0:T(8,128)(2,1)S(1)}, u32[]{:S(2)}, u32[]{:S(2)}) %collective-permute-start.2) | collective-permute-done | bytes 524320 | tf_op jit(solution)/shard_map/ppermute | solution.py:63
  65.5 1.8 collective-permute-start.4
  68.3 2.8 collective-permute-done.14.refs_7_
  71.1 2.6 collective-permute-done.15.refs_8_
  73.7 7.2 %shard_map.136 = (bf16[512,512]{1,0:T(8,128)(2,1)S(1)}, f32[1,512]{1,0:T(1,128)S(1)}, bf16[1024,4096]{1,0:T(8,128)(2,1)}, bf16[2048,1024]{1,0:T(8,128)(2,1)}) custom-call(s32[9]{0:T(128)S(1)} %pad_add_fusion.ring_ref, bf16[512,512]{1,0:T(8,128)(2,1)S(1)} %bitcast.44, bf16[512,512]{1,0:T(8,128)(2,1)S(1)} %copy-done.15, bf16[512,512]{1,0:T(8,128)(2,1)S(1)} %copy-done.17, ...), custom_call_target="tpu_custom_call" | custom-call | flops 2147483648 | bytes 12582912 | tf_op jit(solution)/shard_map/pallas_call | solution.py:164
  85.2 10.6 %collective-permute-done.19.refs_1_ = bf16[512,512]{1,0:T(8,128)(2,1)S(1)} collective-permute-done((bf16[512,512]{1,0:T(8,128)(2,1)S(1)}, bf16[512,512]{1,0:T(8,128)(2,1)S(1)}, u32[]{:S(2)}, u32[]{:S(2)}) %collective-permute-start.19) | collective-permute-done | bytes 524320 | tf_op jit(solution)/shard_map/ppermute | solution.py:63
  97.8 3.6 collective-permute-done.6.refs_7_
  103.0 6.3 %shard_map.137 = (bf16[512,512]{1,0:T(8,128)(2,1)S(1)}, f32[1,512]{1,0:T(1,128)S(1)}, bf16[1024,4096]{1,0:T(8,128)(2,1)}, bf16[2048,1024]{1,0:T(8,128)(2,1)}) custom-call(s32[9]{0:T(128)S(1)} %pad_add_fusion.ring_ref, bf16[512,512]{1,0:T(8,128)(2,1)S(1)} %bitcast.41, ...), custom_call_target="tpu_custom_call", output_to_operand_aliasing={{2}: (12, {}), {3}: (13, {})} | custom-call | flops 2147483648 | bytes 12582912 | tf_op jit(solution)/shard_map/pallas_call | solution.py:164
  114.7 9.6 %collective-permute-done.27.refs_1_ = bf16[512,512]{1,0:T(8,128)(2,1)S(1)} collective-permute-done((bf16[512,512]{1,0:T(8,128)(2,1)S(1)}, bf16[512,512]{1,0:T(8,128)(2,1)S(1)}, u32[]{:S(2)}, u32[]{:S(2)}) %collective-permute-start.27) | collective-permute-done | bytes 524320 | tf_op jit(solution)/shard_map/ppermute | solution.py:63
  126.3 9.2 %collective-permute-done.23.refs_5_ = bf16[512,512]{1,0:T(8,128)(2,1)S(1)} collective-permute-done((bf16[512,512]{1,0:T(8,128)(2,1)S(1)}, bf16[512,512]{1,0:T(8,128)(2,1)S(1)}, u32[]{:S(2)}, u32[]{:S(2)}) %collective-permute-start.23) | collective-permute-done | bytes 524320 | tf_op jit(solution)/shard_map/ppermute | solution.py:63
  138.1 8.6 %collective-permute-done.29.refs_3_ = bf16[512,512]{1,0:T(8,128)(2,1)S(1)} collective-permute-done((bf16[512,512]{1,0:T(8,128)(2,1)S(1)}, bf16[512,512]{1,0:T(8,128)(2,1)S(1)}, u32[]{:S(2)}, u32[]{:S(2)}) %collective-permute-start.29) | collective-permute-done | bytes 524320 | tf_op jit(solution)/shard_map/ppermute | solution.py:63
  148.8 3.6 collective-permute-done.25.refs_7_
  153.9 12.5 %shard_map.139 = (f32[1600,512]{1,0:T(8,128)}, f32[2,512]{1,0:T(2,128)S(1)}, f32[1600,128]{1,0:T(8,128)S(1)}, bf16[1024,4096]{1,0:T(8,128)(2,1)}, bf16[2048,1024]{1,0:T(8,128)(2,1)}) custom-call(s32[9]{0:T(128)S(1)} %pad_add_fusion.ring_ref, bf16[512,512]{1,0:T(8,128)(2,1)S(1)} %get-tuple-element.32.refs_0_, ...), custom_call_target="tpu_custom_call" | custom-call | flops 6710886400 | bytes 26411008 | tf_op jit(solution)/shard_map/pallas_call | solution.py:234
  167.0 3.2 collective-permute-done.35
  172.3 1.8 collective-permute-start.34
  175.7 4.0 %collective-permute-done.37 = f32[2,512]{1,0:T(2,128)S(1)} collective-permute-done((f32[2,512]{1,0:T(2,128)S(1)}, f32[2,512]{1,0:T(2,128)S(1)}, u32[]{:S(2)}, u32[]{:S(2)}) %collective-permute-start.37) | collective-permute-done | bytes 4128 | tf_op jit(solution)/shard_map/ppermute | solution.py:434
  179.7 5.7 %shard_map.140.refs_0_ = bf16[8,1600,128]{2,1,0:T(8,128)(2,1)S(1)} custom-call(s32[8]{0:T(128)S(1)} %select_reduce_fusion.source_ref, s32[8]{0:T(128)S(1)} %convert_element_type.19.present_ref, f32[1600,512]{1,0:T(8,128)} %get-tuple-element.37.gained_ref, bf16[1600,1024]{1,0:T(8,128)(2,1)} %bitcast.28, f32[2,512]{1,0:T(2,128)S(1)} %add_multiply_fusion.2.means_ref.refs_1_, ...), custom_call_target="tpu_custom_call" | custom-call | flops 9830400 | bytes 13107200 | tf_op jit(solution)/shard_map/pallas_call | solution.py:374
  187.1 12.5 %shard_map.142 = (f32[1600,512]{1,0:T(8,128)}, f32[2,512]{1,0:T(2,128)S(1)}, f32[1600,128]{1,0:T(8,128)S(1)}, bf16[1024,4096]{1,0:T(8,128)(2,1)}, bf16[2048,1024]{1,0:T(8,128)(2,1)}) custom-call(s32[9]{0:T(128)S(1)} %pad_add_fusion.ring_ref, bf16[512,512]{1,0:T(8,128)(2,1)S(1)} %get-tuple-element.34.refs_0_, ...), custom_call_target="tpu_custom_call", output_to_operand_aliasing={{3}: (16, {}), {4}: (17, {})} | custom-call | flops 6710886400 | bytes 26411008 | tf_op jit(solution)/shard_map/pallas_call | solution.py:234
  200.5 4.8 %all-to-all-start.1 = ((bf16[8,1600,128]{2,1,0:T(8,128)(2,1)}), bf16[8,1600,128]{2,1,0:T(8,128)(2,1)}, u32[]{:S(2)}, u32[]{:S(2)}) async-start(bf16[8,1600,128]{2,1,0:T(8,128)(2,1)} %copy-done.1), calls=%async_computation.1 | async-start | bytes 6553600 | tf_op jit(solution)/shard_map/all_to_all | solution.py:555
  205.8 6.6 %collective-permute-done.38.a_other_ref = bf16[1600,1024]{1,0:T(8,128)(2,1)} collective-permute-done((bf16[1600,1024]{1,0:T(8,128)(2,1)S(1)}, bf16[1600,1024]{1,0:T(8,128)(2,1)}, u32[]{:S(2)}, u32[]{:S(2)}) %collective-permute-start.38) | collective-permute-done | bytes 3276832 | tf_op jit(solution)/shard_map/ppermute | solution.py:426
  212.4 6.3 %shard_map.143.refs_1_ = bf16[800,1024]{1,0:T(8,128)(2,1)S(1)} custom-call(s32[1]{0:T(128)} %bitcast.6.member_ref, bf16[1600,1024]{1,0:T(8,128)(2,1)S(1)} %bitcast.36, bf16[1600,1024]{1,0:T(8,128)(2,1)} %collective-permute-done.38.a_other_ref, bf16[1024,4096]{1,0:T(8,128)(2,1)} %get-tuple-element.41.b_ref, bf16[2048,1024]{1,0:T(8,128)(2,1)} %collective-permute-done.39.b_other_ref), custom_call_target="tpu_custom_call" | custom-call | flops 3355443200 | bytes 10747904 | tf_op jit(solution)/shard_map/pallas_call | solution.py:297
  220.4 12.4 %collective-permute-done.44 = f32[2,512]{1,0:T(2,128)S(1)} collective-permute-done((f32[2,512]{1,0:T(2,128)S(1)}, f32[2,512]{1,0:T(2,128)S(1)}, u32[]{:S(2)}, u32[]{:S(2)}) %collective-permute-start.44) | collective-permute-done | bytes 4128 | tf_op jit(solution)/shard_map/ppermute | solution.py:434
  232.8 1.6 collective-permute-start.45
  234.4 25.9 %collective-permute-done.45 = f32[2,512]{1,0:T(2,128)S(1)} collective-permute-done((f32[2,512]{1,0:T(2,128)S(1)}, f32[2,512]{1,0:T(2,128)S(1)}, u32[]{:S(2)}, u32[]{:S(2)}) %collective-permute-start.45) | collective-permute-done | bytes 4128 | tf_op jit(solution)/shard_map/ppermute | solution.py:434
  260.3 6.3 %shard_map.144.refs_2_ = bf16[800,1024]{1,0:T(8,128)(2,1)S(1)} custom-call(s32[1]{0:T(128)} %bitcast.6.member_ref, bf16[1600,1024]{1,0:T(8,128)(2,1)S(1)} %bitcast.37, bf16[1600,1024]{1,0:T(8,128)(2,1)} %collective-permute-done.38.a_other_ref, bf16[1024,4096]{1,0:T(8,128)(2,1)} %get-tuple-element.41.b_ref, bf16[2048,1024]{1,0:T(8,128)(2,1)} %collective-permute-done.39.b_other_ref), custom_call_target="tpu_custom_call" | custom-call | flops 3355443200 | bytes 10747904 | tf_op jit(solution)/shard_map/pallas_call | solution.py:297
  267.8 3.3 collective-permute-start.46
  271.2 8.7 %collective-permute-done.46 = f32[2,512]{1,0:T(2,128)S(1)} collective-permute-done((f32[2,512]{1,0:T(2,128)S(1)}, f32[2,512]{1,0:T(2,128)S(1)}, u32[]{:S(2)}, u32[]{:S(2)}) %collective-permute-start.46) | collective-permute-done | bytes 4128 | tf_op jit(solution)/shard_map/ppermute | solution.py:434
  279.8 7.6 %shard_map.149.refs_0_ = bf16[8,1600,128]{2,1,0:T(8,128)(2,1)} custom-call(s32[8]{0:T(128)S(1)} %select_reduce_fusion.source_ref, s32[8]{0:T(128)S(1)} %convert_element_type.19.present_ref, f32[1600,512]{1,0:T(8,128)} %get-tuple-element.43.gained_ref, bf16[1600,1024]{1,0:T(8,128)(2,1)} %bitcast.33, f32[2,512]{1,0:T(2,128)S(1)} %add_multiply_fusion.1.means_ref, ...), custom_call_target="tpu_custom_call" | custom-call | flops 9830400 | bytes 13107200 | tf_op jit(solution)/shard_map/pallas_call | solution.py:374
  288.6 3.7 all-to-all-start
  296.9 5.7 %shard_map.138 = bf16[1024,512]{1,0:T(8,128)(2,1)} custom-call(s32[1]{0:T(128)} %bitcast.6.member_ref, bf16[1024,4096]{1,0:T(8,128)(2,1)} %get-tuple-element.28.a_ref, bf16[2048,1024]{1,0:T(8,128)(2,1)} %collective-permute-done.16.a_other_ref, bf16[1024,512]{1,0:T(8,128)(2,1)S(1)} %copy-done.4, bf16[1024,512]{1,0:T(8,128)(2,1)S(1)} %collective-permute-done.17.b_other_ref), custom_call_target="tpu_custom_call" | custom-call | flops 2147483648 | bytes 8388608 | tf_op jit(solution)/shard_map/pallas_call | solution.py:297
  306.1 5.7 %shard_map.151.refs_0_ = bf16[256,12800]{1,0:T(8,128)(2,1)} custom-call(bf16[12800,128]{1,0:T(8,128)(2,1)} %bitcast.17.in_ref), custom_call_target="tpu_custom_call" | custom-call | bytes 6553600 | tf_op jit(solution)/shard_map/pallas_call | solution.py:411
  311.8 19.6 %collective-permute-done.41.refs_2_.refs_1_ = bf16[800,1024]{1,0:T(8,128)(2,1)} collective-permute-done((bf16[800,1024]{1,0:T(8,128)(2,1)}, bf16[800,1024]{1,0:T(8,128)(2,1)}, u32[]{:S(2)}, u32[]{:S(2)}) %collective-permute-start.41) | collective-permute-done | bytes 1638432 | tf_op jit(solution)/shard_map/ppermute | solution.py:330
  331.4 12.6 %shard_map.147.refs_1_ = f32[1600,1024]{1,0:T(8,128)} custom-call(s32[1]{0:T(128)} %bitcast.member_ref, bf16[1600,1024]{1,0:T(8,128)(2,1)} %bitcast.34, bf16[1600,1024]{1,0:T(8,128)(2,1)} %collective-permute-done.38.a_other_ref, bf16[1024,4096]{1,0:T(8,128)(2,1)} %get-tuple-element.41.b_ref, bf16[2048,1024]{1,0:T(8,128)(2,1)} %collective-permute-done.39.b_other_ref, ...), custom_call_target="tpu_custom_call" | custom-call | flops 6710886400 | bytes 17301504 | tf_op jit(solution)/shard_map/pallas_call | solution.py:297
  345.1 8.5 %collective-permute-done.18.refs_0_ = bf16[1024,512]{1,0:T(8,128)(2,1)} collective-permute-done((bf16[1024,512]{1,0:T(8,128)(2,1)}, bf16[1024,512]{1,0:T(8,128)(2,1)}, u32[]{:S(2)}, u32[]{:S(2)}) %collective-permute-start.18) | collective-permute-done | bytes 1048608 | tf_op jit(solution)/shard_map/ppermute | solution.py:330
  353.6 5.9 %shard_map.146.refs_2_ = f32[1024,512]{1,0:T(8,128)} custom-call(s32[1]{0:T(128)} %bitcast.member_ref, bf16[1024,4096]{1,0:T(8,128)(2,1)} %get-tuple-element.28.a_ref, bf16[2048,1024]{1,0:T(8,128)(2,1)} %collective-permute-done.16.a_other_ref, bf16[1024,512]{1,0:T(8,128)(2,1)S(1)} %copy-done.5, bf16[1024,512]{1,0:T(8,128)(2,1)S(1)} %copy-done.9, ...), custom_call_target="tpu_custom_call" | custom-call | flops 2147483648 | bytes 8388608 | tf_op jit(solution)/shard_map/pallas_call | solution.py:297
  360.8 5.1 %all-to-all-done = bf16[8,1600,128]{2,1,0:T(8,128)(2,1)S(1)} async-done(((bf16[8,1600,128]{2,1,0:T(8,128)(2,1)}), bf16[8,1600,128]{2,1,0:T(8,128)(2,1)S(1)}, u32[]{:S(2)}, u32[]{:S(2)}) %all-to-all-start) | async-done | bytes 3276832 | tf_op jit(solution)/shard_map/all_to_all | solution.py:555
  367.5 3.2 shard_map.152
  (144 shorter events, 53.3 us)
Async XLA Ops:
  1.9 14.9 %collective-permute-start.8 = (bf16[512,512]{1,0:T(8,128)(2,1)S(1)}, bf16[512,512]{1,0:T(8,128)(2,1)S(1)}, u32[]{:S(2)}, u32[]{:S(2)}) collective-permute-start(bf16[512,512]{1,0:T(8,128)(2,1)S(1)} %bitcast.42), channel_id=1, source_target_pairs={{0,2},{2,4},{4,6},{6,7},{7,5},{5,3},{3,1},{1,0},{8,10},{10,12},{12... | collective-permute-start | bytes 1572872 | tf_op jit(solution)/shard_map/ppermute | solution.py:63
  5.0 14.5 %collective-permute-start.9 = (bf16[512,512]{1,0:T(8,128)(2,1)S(1)}, bf16[512,512]{1,0:T(8,128)(2,1)S(1)}, u32[]{:S(2)}, u32[]{:S(2)}) collective-permute-start(bf16[512,512]{1,0:T(8,128)(2,1)S(1)} %bitcast.43), channel_id=1, source_target_pairs={{0,1},{2,0},{4,2},{6,4},{7,6},{5,7},{3,5},{1,3},{8,9},{10,8},{12,1... | collective-permute-start | bytes 1572872 | tf_op jit(solution)/shard_map/ppermute | solution.py:64
  16.9 15.0 %collective-permute-start.10 = (bf16[512,512]{1,0:T(8,128)(2,1)S(1)}, bf16[512,512]{1,0:T(8,128)(2,1)}, u32[]{:S(2)}, u32[]{:S(2)}) collective-permute-start(bf16[512,512]{1,0:T(8,128)(2,1)S(1)} %collective-permute-done.8.refs_1_), channel_id=1, source_target_pairs={{0,2},{2,4},{4,6},{6,7},{7,5},{5,3},{3,1},{1,0},{8,10},{10,12},{12... | collective-permute-start | bytes 1572872 | tf_op jit(solution)/shard_map/ppermute | solution.py:63
  19.5 15.0 %collective-permute-start.11 = (bf16[512,512]{1,0:T(8,128)(2,1)S(1)}, bf16[512,512]{1,0:T(8,128)(2,1)}, u32[]{:S(2)}, u32[]{:S(2)}) collective-permute-start(bf16[512,512]{1,0:T(8,128)(2,1)S(1)} %collective-permute-done.9.refs_2_), channel_id=1, source_target_pairs={{0,1},{2,0},{4,2},{6,4},{7,6},{5,7},{3,5},{1,3},{8,9},{10,8},{12,1... | collective-permute-start | bytes 1572872 | tf_op jit(solution)/shard_map/ppermute | solution.py:64
  20.5 22.5 %collective-permute-start = (bf16[512,512]{1,0:T(8,128)(2,1)S(1)}, bf16[512,512]{1,0:T(8,128)(2,1)S(1)}, u32[]{:S(2)}, u32[]{:S(2)}) collective-permute-start(bf16[512,512]{1,0:T(8,128)(2,1)S(1)} %bitcast.39), channel_id=1, source_target_pairs={{0,2},{2,4},{4,6},{6,7},{7,5},{5,3},{3,1},{1,0},{8,10},{10,12},{12... | collective-permute-start | bytes 1572872 | tf_op jit(solution)/shard_map/ppermute | solution.py:63
  22.3 23.3 %collective-permute-start.1 = (bf16[512,512]{1,0:T(8,128)(2,1)S(1)}, bf16[512,512]{1,0:T(8,128)(2,1)S(1)}, u32[]{:S(2)}, u32[]{:S(2)}) collective-permute-start(bf16[512,512]{1,0:T(8,128)(2,1)S(1)} %bitcast.40), channel_id=1, source_target_pairs={{0,1},{2,0},{4,2},{6,4},{7,6},{5,7},{3,5},{1,3},{8,9},{10,8},{12,1... | collective-permute-start | bytes 1572872 | tf_op jit(solution)/shard_map/ppermute | solution.py:64
  31.9 22.4 %collective-permute-start.12 = (bf16[512,512]{1,0:T(8,128)(2,1)}, bf16[512,512]{1,0:T(8,128)(2,1)S(1)}, u32[]{:S(2)}, u32[]{:S(2)}) collective-permute-start(bf16[512,512]{1,0:T(8,128)(2,1)} %collective-permute-done.10.refs_3_), channel_id=1, source_target_pairs={{0,2},{2,4},{4,6},{6,7},{7,5},{5,3},{3,1},{1,0},{8,10},{10,12},{12... | collective-permute-start | bytes 1572872 | tf_op jit(solution)/shard_map/ppermute | solution.py:63
  34.4 22.4 %collective-permute-start.13 = (bf16[512,512]{1,0:T(8,128)(2,1)}, bf16[512,512]{1,0:T(8,128)(2,1)S(1)}, u32[]{:S(2)}, u32[]{:S(2)}) collective-permute-start(bf16[512,512]{1,0:T(8,128)(2,1)} %collective-permute-done.11.refs_4_), channel_id=1, source_target_pairs={{0,1},{2,0},{4,2},{6,4},{7,6},{5,7},{3,5},{1,3},{8,9},{10,8},{12,1... | collective-permute-start | bytes 1572872 | tf_op jit(solution)/shard_map/ppermute | solution.py:64
  43.0 22.5 %collective-permute-start.2 = (bf16[512,512]{1,0:T(8,128)(2,1)S(1)}, bf16[512,512]{1,0:T(8,128)(2,1)S(1)}, u32[]{:S(2)}, u32[]{:S(2)}) collective-permute-start(bf16[512,512]{1,0:T(8,128)(2,1)S(1)} %collective-permute-done.refs_1_), channel_id=1, source_target_pairs={{0,2},{2,4},{4,6},{6,7},{7,5},{5,3},{3,1},{1,0},{8,10},{10,12},{12... | collective-permute-start | bytes 1572872 | tf_op jit(solution)/shard_map/ppermute | solution.py:63
  45.6 22.5 %collective-permute-start.3 = (bf16[512,512]{1,0:T(8,128)(2,1)S(1)}, bf16[512,512]{1,0:T(8,128)(2,1)S(1)}, u32[]{:S(2)}, u32[]{:S(2)}) collective-permute-start(bf16[512,512]{1,0:T(8,128)(2,1)S(1)} %collective-permute-done.1.refs_2_), channel_id=1, source_target_pairs={{0,1},{2,0},{4,2},{6,4},{7,6},{5,7},{3,5},{1,3},{8,9},{10,8},{12,1... | collective-permute-start | bytes 1572872 | tf_op jit(solution)/shard_map/ppermute | solution.py:64
  54.2 16.8 %collective-permute-start.14 = (bf16[256,512]{1,0:T(8,128)(2,1)S(1)}, bf16[256,512]{1,0:T(8,128)(2,1)S(1)}, u32[]{:S(2)}, u32[]{:S(2)}) collective-permute-start(bf16[256,512]{1,0:T(8,128)(2,1)S(1)} %slice.60), channel_id=1, source_target_pairs={{0,2},{2,4},{4,6},{6,7},{7,5},{5,3},{3,1},{1,0},{8,10},{10,12},{12... | collective-permute-start | bytes 786440 | tf_op jit(solution)/shard_map/ppermute | solution.py:67
  56.8 16.8 %collective-permute-start.15 = (bf16[256,512]{1,0:T(8,128)(2,1)S(1)}, bf16[256,512]{1,0:T(8,128)(2,1)S(1)}, u32[]{:S(2)}, u32[]{:S(2)}) collective-permute-start(bf16[256,512]{1,0:T(8,128)(2,1)S(1)} %slice.61), channel_id=1, source_target_pairs={{0,1},{2,0},{4,2},{6,4},{7,6},{5,7},{3,5},{1,3},{8,9},{10,8},{12,1... | collective-permute-start | bytes 786440 | tf_op jit(solution)/shard_map/ppermute | solution.py:68
  65.5 17.5 %collective-permute-start.4 = (bf16[512,512]{1,0:T(8,128)(2,1)S(1)}, bf16[512,512]{1,0:T(8,128)(2,1)S(1)}, u32[]{:S(2)}, u32[]{:S(2)}) collective-permute-start(bf16[512,512]{1,0:T(8,128)(2,1)S(1)} %collective-permute-done.2.refs_3_), channel_id=1, source_target_pairs={{0,2},{2,4},{4,6},{6,7},{7,5},{5,3},{3,1},{1,0},{8,10},{10,12},{12... | collective-permute-start | bytes 1572872 | tf_op jit(solution)/shard_map/ppermute | solution.py:63
  68.1 16.8 %collective-permute-start.5 = (bf16[512,512]{1,0:T(8,128)(2,1)S(1)}, bf16[512,512]{1,0:T(8,128)(2,1)S(1)}, u32[]{:S(2)}, u32[]{:S(2)}) collective-permute-start(bf16[512,512]{1,0:T(8,128)(2,1)S(1)} %collective-permute-done.3.refs_4_), channel_id=1, source_target_pairs={{0,1},{2,0},{4,2},{6,4},{7,6},{5,7},{3,5},{1,3},{8,9},{10,8},{12,1... | collective-permute-start | bytes 1572872 | tf_op jit(solution)/shard_map/ppermute | solution.py:64
  80.9 14.9 %collective-permute-start.19 = (bf16[512,512]{1,0:T(8,128)(2,1)S(1)}, bf16[512,512]{1,0:T(8,128)(2,1)S(1)}, u32[]{:S(2)}, u32[]{:S(2)}) collective-permute-start(bf16[512,512]{1,0:T(8,128)(2,1)S(1)} %get-tuple-element.32.refs_0_), channel_id=1, source_target_pairs={{0,2},{2,4},{4,6},{6,7},{7,5},{5,3},{3,1},{1,0},{8,10},{10,12},{12... | collective-permute-start | bytes 1572872 | tf_op jit(solution)/shard_map/ppermute | solution.py:63
  82.5 14.9 %collective-permute-start.20 = (bf16[512,512]{1,0:T(8,128)(2,1)S(1)}, bf16[512,512]{1,0:T(8,128)(2,1)S(1)}, u32[]{:S(2)}, u32[]{:S(2)}) collective-permute-start(bf16[512,512]{1,0:T(8,128)(2,1)S(1)} %get-tuple-element.32.refs_0_), channel_id=1, source_target_pairs={{0,1},{2,0},{4,2},{6,4},{7,6},{5,7},{3,5},{1,3},{8,9},{10,8},{12,1... | collective-permute-start | bytes 1572872 | tf_op jit(solution)/shard_map/ppermute | solution.py:64
  83.0 18.4 %collective-permute-start.6 = (bf16[256,512]{1,0:T(8,128)(2,1)S(1)}, bf16[256,512]{1,0:T(8,128)(2,1)S(1)}, u32[]{:S(2)}, u32[]{:S(2)}) collective-permute-start(bf16[256,512]{1,0:T(8,128)(2,1)S(1)} %slice.57), channel_id=1, source_target_pairs={{0,2},{2,4},{4,6},{6,7},{7,5},{5,3},{3,1},{1,0},{8,10},{10,12},{12... | collective-permute-start | bytes 786440 | tf_op jit(solution)/shard_map/ppermute | solution.py:67
  84.8 18.2 %collective-permute-start.7 = (bf16[256,512]{1,0:T(8,128)(2,1)S(1)}, bf16[256,512]{1,0:T(8,128)(2,1)S(1)}, u32[]{:S(2)}, u32[]{:S(2)}) collective-permute-start(bf16[256,512]{1,0:T(8,128)(2,1)S(1)} %slice.58), channel_id=1, source_target_pairs={{0,1},{2,0},{4,2},{6,4},{7,6},{5,7},{3,5},{1,3},{8,9},{10,8},{12,1... | collective-permute-start | bytes 786440 | tf_op jit(solution)/shard_map/ppermute | solution.py:68
  95.8 16.5 %collective-permute-start.21 = (bf16[512,512]{1,0:T(8,128)(2,1)S(1)}, bf16[512,512]{1,0:T(8,128)(2,1)S(1)}, u32[]{:S(2)}, u32[]{:S(2)}) collective-permute-start(bf16[512,512]{1,0:T(8,128)(2,1)S(1)} %collective-permute-done.19.refs_1_), channel_id=1, source_target_pairs={{0,2},{2,4},{4,6},{6,7},{7,5},{5,3},{3,1},{1,0},{8,10},{10,12},{12... | collective-permute-start | bytes 1572872 | tf_op jit(solution)/shard_map/ppermute | solution.py:63
  97.4 16.9 %collective-permute-start.22 = (bf16[512,512]{1,0:T(8,128)(2,1)S(1)}, bf16[512,512]{1,0:T(8,128)(2,1)S(1)}, u32[]{:S(2)}, u32[]{:S(2)}) collective-permute-start(bf16[512,512]{1,0:T(8,128)(2,1)S(1)} %collective-permute-done.20.refs_2_), channel_id=1, source_target_pairs={{0,1},{2,0},{4,2},{6,4},{7,6},{5,7},{3,5},{1,3},{8,9},{10,8},{12,1... | collective-permute-start | bytes 1572872 | tf_op jit(solution)/shard_map/ppermute | solution.py:64
  109.3 14.9 %collective-permute-start.27 = (bf16[512,512]{1,0:T(8,128)(2,1)S(1)}, bf16[512,512]{1,0:T(8,128)(2,1)S(1)}, u32[]{:S(2)}, u32[]{:S(2)}) collective-permute-start(bf16[512,512]{1,0:T(8,128)(2,1)S(1)} %get-tuple-element.34.refs_0_), channel_id=1, source_target_pairs={{0,2},{2,4},{4,6},{6,7},{7,5},{5,3},{3,1},{1,0},{8,10},{10,12},{12... | collective-permute-start | bytes 1572872 | tf_op jit(solution)/shard_map/ppermute | solution.py:63
  111.0 14.9 %collective-permute-start.28 = (bf16[512,512]{1,0:T(8,128)(2,1)S(1)}, bf16[512,512]{1,0:T(8,128)(2,1)S(1)}, u32[]{:S(2)}, u32[]{:S(2)}) collective-permute-start(bf16[512,512]{1,0:T(8,128)(2,1)S(1)} %get-tuple-element.34.refs_0_), channel_id=1, source_target_pairs={{0,1},{2,0},{4,2},{6,4},{7,6},{5,7},{3,5},{1,3},{8,9},{10,8},{12,1... | collective-permute-start | bytes 1572872 | tf_op jit(solution)/shard_map/ppermute | solution.py:64
  112.3 23.2 %collective-permute-start.23 = (bf16[512,512]{1,0:T(8,128)(2,1)S(1)}, bf16[512,512]{1,0:T(8,128)(2,1)S(1)}, u32[]{:S(2)}, u32[]{:S(2)}) collective-permute-start(bf16[512,512]{1,0:T(8,128)(2,1)S(1)} %collective-permute-done.21.refs_3_), channel_id=1, source_target_pairs={{0,2},{2,4},{4,6},{6,7},{7,5},{5,3},{3,1},{1,0},{8,10},{10,12},{12... | collective-permute-start | bytes 1572872 | tf_op jit(solution)/shard_map/ppermute | solution.py:63
  114.2 22.9 %collective-permute-start.24 = (bf16[512,512]{1,0:T(8,128)(2,1)S(1)}, bf16[512,512]{1,0:T(8,128)(2,1)S(1)}, u32[]{:S(2)}, u32[]{:S(2)}) collective-permute-start(bf16[512,512]{1,0:T(8,128)(2,1)S(1)} %collective-permute-done.22.refs_4_), channel_id=1, source_target_pairs={{0,1},{2,0},{4,2},{6,4},{7,6},{5,7},{3,5},{1,3},{8,9},{10,8},{12,1... | collective-permute-start | bytes 1572872 | tf_op jit(solution)/shard_map/ppermute | solution.py:64
  124.3 22.5 %collective-permute-start.29 = (bf16[512,512]{1,0:T(8,128)(2,1)S(1)}, bf16[512,512]{1,0:T(8,128)(2,1)S(1)}, u32[]{:S(2)}, u32[]{:S(2)}) collective-permute-start(bf16[512,512]{1,0:T(8,128)(2,1)S(1)} %collective-permute-done.27.refs_1_), channel_id=1, source_target_pairs={{0,2},{2,4},{4,6},{6,7},{7,5},{5,3},{3,1},{1,0},{8,10},{10,12},{12... | collective-permute-start | bytes 1572872 | tf_op jit(solution)/shard_map/ppermute | solution.py:63
  125.8 22.5 %collective-permute-start.30 = (bf16[512,512]{1,0:T(8,128)(2,1)S(1)}, bf16[512,512]{1,0:T(8,128)(2,1)S(1)}, u32[]{:S(2)}, u32[]{:S(2)}) collective-permute-start(bf16[512,512]{1,0:T(8,128)(2,1)S(1)} %collective-permute-done.28.refs_2_), channel_id=1, source_target_pairs={{0,1},{2,0},{4,2},{6,4},{7,6},{5,7},{3,5},{1,3},{8,9},{10,8},{12,1... | collective-permute-start | bytes 1572872 | tf_op jit(solution)/shard_map/ppermute | solution.py:64
  135.5 16.8 %collective-permute-start.25 = (bf16[256,512]{1,0:T(8,128)(2,1)S(1)}, bf16[256,512]{1,0:T(8,128)(2,1)S(1)}, u32[]{:S(2)}, u32[]{:S(2)}) collective-permute-start(bf16[256,512]{1,0:T(8,128)(2,1)S(1)} %slice.62), channel_id=1, source_target_pairs={{0,2},{2,4},{4,6},{6,7},{7,5},{5,3},{3,1},{1,0},{8,10},{10,12},{12... | collective-permute-start | bytes 786440 | tf_op jit(solution)/shard_map/ppermute | solution.py:67
  137.2 16.8 %collective-permute-start.26 = (bf16[256,512]{1,0:T(8,128)(2,1)S(1)}, bf16[256,512]{1,0:T(8,128)(2,1)S(1)}, u32[]{:S(2)}, u32[]{:S(2)}) collective-permute-start(bf16[256,512]{1,0:T(8,128)(2,1)S(1)} %slice.63), channel_id=1, source_target_pairs={{0,1},{2,0},{4,2},{6,4},{7,6},{5,7},{3,5},{1,3},{8,9},{10,8},{12,1... | collective-permute-start | bytes 786440 | tf_op jit(solution)/shard_map/ppermute | solution.py:68
  146.7 25.0 %collective-permute-start.31 = (bf16[512,512]{1,0:T(8,128)(2,1)S(1)}, bf16[512,512]{1,0:T(8,128)(2,1)S(1)}, u32[]{:S(2)}, u32[]{:S(2)}) collective-permute-start(bf16[512,512]{1,0:T(8,128)(2,1)S(1)} %collective-permute-done.29.refs_3_), channel_id=1, source_target_pairs={{0,2},{2,4},{4,6},{6,7},{7,5},{5,3},{3,1},{1,0},{8,10},{10,12},{12... | collective-permute-start | bytes 1572872 | tf_op jit(solution)/shard_map/ppermute | solution.py:63
  148.3 24.0 %collective-permute-start.32 = (bf16[512,512]{1,0:T(8,128)(2,1)S(1)}, bf16[512,512]{1,0:T(8,128)(2,1)S(1)}, u32[]{:S(2)}, u32[]{:S(2)}) collective-permute-start(bf16[512,512]{1,0:T(8,128)(2,1)S(1)} %collective-permute-done.30.refs_4_), channel_id=1, source_target_pairs={{0,1},{2,0},{4,2},{6,4},{7,6},{5,7},{3,5},{1,3},{8,9},{10,8},{12,1... | collective-permute-start | bytes 1572872 | tf_op jit(solution)/shard_map/ppermute | solution.py:64
  166.4 3.7 collective-permute-start.35
  170.1 4.0 %collective-permute-start.36 = (f32[2,512]{1,0:T(2,128)S(1)}, f32[2,512]{1,0:T(2,128)S(1)}, u32[]{:S(2)}, u32[]{:S(2)}) collective-permute-start(f32[2,512]{1,0:T(2,128)S(1)} %add.73), channel_id=1, source_target_pairs={{0,2},{1,3},{2,0},{3,1},{4,6},{5,7},{6,4},{7,5},{8,10},{9,11},{10,... | collective-permute-start | bytes 12296 | tf_op jit(solution)/shard_map/ppermute | solution.py:434
  171.7 13.7 %collective-permute-start.33 = (bf16[256,512]{1,0:T(8,128)(2,1)S(1)}, bf16[256,512]{1,0:T(8,128)(2,1)S(1)}, u32[]{:S(2)}, u32[]{:S(2)}) collective-permute-start(bf16[256,512]{1,0:T(8,128)(2,1)S(1)} %slice.64), channel_id=1, source_target_pairs={{0,2},{2,4},{4,6},{6,7},{7,5},{5,3},{3,1},{1,0},{8,10},{10,12},{12... | collective-permute-start | bytes 786440 | tf_op jit(solution)/shard_map/ppermute | solution.py:67
  172.3 13.1 %collective-permute-start.34 = (bf16[256,512]{1,0:T(8,128)(2,1)S(1)}, bf16[256,512]{1,0:T(8,128)(2,1)S(1)}, u32[]{:S(2)}, u32[]{:S(2)}) collective-permute-start(bf16[256,512]{1,0:T(8,128)(2,1)S(1)} %slice.65), channel_id=1, source_target_pairs={{0,1},{2,0},{4,2},{6,4},{7,6},{5,7},{3,5},{1,3},{8,9},{10,8},{12,1... | collective-permute-start | bytes 786440 | tf_op jit(solution)/shard_map/ppermute | solution.py:68
  174.1 5.6 %collective-permute-start.37 = (f32[2,512]{1,0:T(2,128)S(1)}, f32[2,512]{1,0:T(2,128)S(1)}, u32[]{:S(2)}, u32[]{:S(2)}) collective-permute-start(f32[2,512]{1,0:T(2,128)S(1)} %add.74), channel_id=1, source_target_pairs={{0,4},{1,5},{2,6},{3,7},{4,0},{5,1},{6,2},{7,3},{8,12},{9,13},{10,... | collective-permute-start | bytes 12296 | tf_op jit(solution)/shard_map/ppermute | solution.py:434
  200.4 12.0 %collective-permute-start.39 = (bf16[2048,1024]{1,0:T(8,128)(2,1)}, bf16[2048,1024]{1,0:T(8,128)(2,1)}, u32[]{:S(2)}, u32[]{:S(2)}) collective-permute-start(bf16[2048,1024]{1,0:T(8,128)(2,1)} %get-tuple-element.42), channel_id=1, source_target_pairs={{0,8},{8,0},{16,24},{24,16},{1,9},{9,1},{17,25},{25,17},{2,10},{10... | collective-permute-start | bytes 12582920 | tf_op jit(solution)/shard_map/ppermute | solution.py:426
  200.5 88.2 %all-to-all-start.1 = ((bf16[8,1600,128]{2,1,0:T(8,128)(2,1)}), bf16[8,1600,128]{2,1,0:T(8,128)(2,1)}, u32[]{:S(2)}, u32[]{:S(2)}) async-start(bf16[8,1600,128]{2,1,0:T(8,128)(2,1)} %copy-done.1), calls=%async_computation.1 | async-start | bytes 6553600 | tf_op jit(solution)/shard_map/all_to_all | solution.py:555
  205.2 7.2 %collective-permute-start.38 = (bf16[1600,1024]{1,0:T(8,128)(2,1)S(1)}, bf16[1600,1024]{1,0:T(8,128)(2,1)}, u32[]{:S(2)}, u32[]{:S(2)}) collective-permute-start(bf16[1600,1024]{1,0:T(8,128)(2,1)S(1)} %bitcast.35), channel_id=1, source_target_pairs={{0,8},{8,0},{16,24},{24,16},{1,9},{9,1},{17,25},{25,17},{2,10},{10... | collective-permute-start | bytes 9830408 | tf_op jit(solution)/shard_map/ppermute | solution.py:426
  218.7 68.8 %collective-permute-start.40 = (bf16[800,1024]{1,0:T(8,128)(2,1)S(1)}, bf16[800,1024]{1,0:T(8,128)(2,1)S(1)}, u32[]{:S(2)}, u32[]{:S(2)}) collective-permute-start(bf16[800,1024]{1,0:T(8,128)(2,1)S(1)} %shard_map.143.refs_1_), channel_id=1, source_target_pairs={{0,16},{8,24},{16,0},{24,8},{1,17},{9,25},{17,1},{25,9},{2,18},{10... | collective-permute-start | bytes 4915208 | tf_op jit(solution)/shard_map/ppermute | solution.py:330
  219.7 75.5 %collective-permute-start.16 = (bf16[2048,1024]{1,0:T(8,128)(2,1)}, bf16[2048,1024]{1,0:T(8,128)(2,1)}, u32[]{:S(2)}, u32[]{:S(2)}) collective-permute-start(bf16[2048,1024]{1,0:T(8,128)(2,1)} %get-tuple-element.29), channel_id=1, source_target_pairs={{0,8},{8,0},{16,24},{24,16},{1,9},{9,1},{17,25},{25,17},{2,10},{10... | collective-permute-start | bytes 12582920 | tf_op jit(solution)/shard_map/ppermute | solution.py:426
  219.7 13.0 %collective-permute-start.44 = (f32[2,512]{1,0:T(2,128)S(1)}, f32[2,512]{1,0:T(2,128)S(1)}, u32[]{:S(2)}, u32[]{:S(2)}) collective-permute-start(f32[2,512]{1,0:T(2,128)S(1)} %get-tuple-element.44), channel_id=1, source_target_pairs={{0,1},{1,0},{2,3},{3,2},{4,5},{5,4},{6,7},{7,6},{8,9},{9,8},{10,11... | collective-permute-start | bytes 12296 | tf_op jit(solution)/shard_map/ppermute | solution.py:434
  232.8 27.5 %collective-permute-start.45 = (f32[2,512]{1,0:T(2,128)S(1)}, f32[2,512]{1,0:T(2,128)S(1)}, u32[]{:S(2)}, u32[]{:S(2)}) collective-permute-start(f32[2,512]{1,0:T(2,128)S(1)} %add.79), channel_id=1, source_target_pairs={{0,2},{1,3},{2,0},{3,1},{4,6},{5,7},{6,4},{7,5},{8,10},{9,11},{10,... | collective-permute-start | bytes 12296 | tf_op jit(solution)/shard_map/ppermute | solution.py:434
  267.8 12.0 %collective-permute-start.46 = (f32[2,512]{1,0:T(2,128)S(1)}, f32[2,512]{1,0:T(2,128)S(1)}, u32[]{:S(2)}, u32[]{:S(2)}) collective-permute-start(f32[2,512]{1,0:T(2,128)S(1)} %shard_map.148), channel_id=1, source_target_pairs={{0,4},{1,5},{2,6},{3,7},{4,0},{5,1},{6,2},{7,3},{8,12},{9,13},{10,... | collective-permute-start | bytes 12296 | tf_op jit(solution)/shard_map/ppermute | solution.py:434
  288.6 77.3 %all-to-all-start = ((bf16[8,1600,128]{2,1,0:T(8,128)(2,1)}), bf16[8,1600,128]{2,1,0:T(8,128)(2,1)S(1)}, u32[]{:S(2)}, u32[]{:S(2)}) async-start(bf16[8,1600,128]{2,1,0:T(8,128)(2,1)} %shard_map.150), calls=%async_computation | async-start | bytes 6553600 | tf_op jit(solution)/shard_map/all_to_all | solution.py:555
  292.4 39.0 %collective-permute-start.41 = (bf16[800,1024]{1,0:T(8,128)(2,1)}, bf16[800,1024]{1,0:T(8,128)(2,1)}, u32[]{:S(2)}, u32[]{:S(2)}) collective-permute-start(bf16[800,1024]{1,0:T(8,128)(2,1)} %copy-done.7), channel_id=1, source_target_pairs={{0,16},{8,24},{16,0},{24,8},{1,17},{9,25},{17,1},{25,9},{2,18},{10... | collective-permute-start | bytes 4915208 | tf_op jit(solution)/shard_map/ppermute | solution.py:330
  302.5 51.1 %collective-permute-start.18 = (bf16[1024,512]{1,0:T(8,128)(2,1)}, bf16[1024,512]{1,0:T(8,128)(2,1)}, u32[]{:S(2)}, u32[]{:S(2)}) collective-permute-start(bf16[1024,512]{1,0:T(8,128)(2,1)} %shard_map.138), channel_id=1, source_target_pairs={{0,16},{8,24},{16,0},{24,8},{1,17},{9,25},{17,1},{25,9},{2,18},{10... | collective-permute-start | bytes 3145736 | tf_op jit(solution)/shard_map/ppermute | solution.py:330
  331.4 12.6 %collective-permute-start.42 = (f32[4224]{0:T(1024)S(1)}, f32[4224]{0:T(1024)S(1)}, u32[]{:S(2)}, u32[]{:S(2)}) collective-permute-start(f32[4224]{0:T(1024)S(1)} %shard_map.145.refs_1_), channel_id=1, source_target_pairs={{0,8},{8,0},{16,24},{24,16},{1,9},{9,1},{17,25},{25,17},{2,10},{10... | collective-permute-start | bytes 50696 | tf_op jit(solution)/shard_map/ppermute | solution.py:434
  344.0 15.5 %collective-permute-start.43 = (f32[4224]{0:T(1024)S(1)}, f32[4224]{0:T(1024)S(1)}, u32[]{:S(2)}, u32[]{:S(2)}) collective-permute-start(f32[4224]{0:T(1024)S(1)} %add.77), channel_id=1, source_target_pairs={{0,16},{8,24},{16,0},{24,8},{1,17},{9,25},{17,1},{25,9},{2,18},{10... | collective-permute-start | bytes 50696 | tf_op jit(solution)/shard_map/ppermute | solution.py:434
  (22 other events, 294.4 us)

commit v2 on v1

--- a/solution.py
+++ b/solution.py
@@ -307,8 +307,8 @@
         out_shape=jax.ShapeDtypeStruct(shape, dtype),
         compiler_params=pltpu.CompilerParams(vmem_limit_bytes=VMEM_LIMIT),
         cost_estimate=pl.CostEstimate(
-            flops=4 * shape[0] * shape[1] * depth,
-            bytes_accessed=4 * depth * (shape[0] + shape[1]) + 4 * shape[0] * shape[1],
+            flops=shape[0] * shape[1] * depth // 4,
+            bytes_accessed=depth * (shape[0] + shape[1]) // 4,
             transcendentals=0,
         ),
     )(
@@ -336,7 +336,7 @@
 
 
 def tie(values, others, place=pl.ANY):
-    spaces = [place] + [pl.ANY] * (len(values) + len(others) - 1)
+    spaces = [place] + [pl.ANY] * (len(values) - 1) + [place] * len(others)
     return pl.pallas_call(
         tie_kernel,
         in_specs=[pl.BlockSpec(memory_space=space) for space in spaces],
@@ -517,13 +517,14 @@
 
     first_gained, first_rows, first_ln, *so_far = norm_of(0, first_backs, (), [])
     first_means = doubling_sum(first_rows, "tp", tp_count) / full_width
-    first_slots, first_means = tie(
-        [slots_of(0, first_gained, first_means), first_means], second_backs[-2:], pltpu.HBM
-    )
-    outgoing = [first_slots]
     second_gained, second_rows, second_ln, backs, backs_swap = norm_of(
         1, second_backs, so_far, [first_means]
     )
+    second_means = doubling_sum(second_rows, "tp", tp_count) / full_width
+    first_slots, second_means = tie(
+        [slots_of(0, first_gained, first_means), second_means], [], pltpu.HBM
+    )
+    first_received = lax.all_to_all(first_slots, "tp", split_axis=0, concat_axis=0, tiled=True)
     backs_other = core_swap(backs_swap, ctx_count)
 
     w1_tile = divisor(width, 400, 16)
@@ -546,13 +547,15 @@
 
     cut = w1_tiles // 2
     spans = [(0, cut), (cut, w1_tiles)] if cut else [(0, w1_tiles)]
-    going_w1, arrived_w1 = chip_products(grad_w1_share, spans, ctx_count, [])
-
-    second_means = doubling_sum(second_rows, "tp", tp_count, going_w1) / full_width
+    _, arrived_w1 = chip_products(grad_w1_share, spans, ctx_count, [second_means])
+
     early = [part for span, part in arrived_w1 if span == spans[0]]
-    outgoing += tie([slots_of(1, second_gained, second_means)], early, pltpu.HBM)
+    (second_slots,) = tie(
+        [slots_of(1, second_gained, second_means)], early + [first_received], pltpu.HBM
+    )
     received = [
-        lax.all_to_all(part, "tp", split_axis=0, concat_axis=0, tiled=True) for part in outgoing
+        first_received,
+        lax.all_to_all(second_slots, "tp", split_axis=0, concat_axis=0, tiled=True),
     ]
     ln_sum = (first_ln + second_ln)[:, :2]
     small = jnp.concatenate(

time: 371 us -> 378 us (1.019)
  waiting for transfers between devices: 195 us -> 203 us
    all_to_all x2, waiting for transfers between devices: 5.12 us -> 54 us  [the longest x1 53.9 us: per_device(): lax.all_to_all(first_slots, 'tp', split_axis=0, concat_axis=0, tiled=True)]
    ppermute x8, waiting for transfers between devices: 54.1 us -> 12.1 us  [doubling_sum(): lax.ppermute(value, axis, [(t, t ^ bit) for t in range(count)])]
    unnamed x42 -> x44, local copies, waits for them, and re-layouts: 9.65 us -> 9.57 us
  transfers between devices with their start and end apart: 49 -> 49, of which waited for: 32 -> 30; matrix products, arithmetic and copies ran while one was open for 3% -> 2% of each run, Pallas kernels for 22% -> 21%
where the time goes in v2:
time: 378 us; the launch traced here: 377 us
  waiting for transfers between devices  203 us (54%)
  Pallas kernels  99.1 us (26%)
  starting transfers between devices  57.1 us (15%)
  local copies, waits for them, and re-layouts  13.6 us (4%)
  other arithmetic  3.95 us (1%)
    ppermute x12, waiting for transfers between devices, ring_blocks(): up = lax.ppermute(up, 'tp', ahead)  81.3 us
    all_to_all x1, waiting for transfers between devices, per_device(): lax.all_to_all(first_slots, 'tp', split_axis=0, concat_axis=0, tiled=True)  53.9 us
    pallas_call x5, Pallas kernels, pair_product(): pl.pallas_call(functools.partial(pair_kernel, contract, scale, [span for...  38.2 us
    ppermute x3, waiting for transfers between devices, chip_products(): arrived.append((span, lax.ppermute(going[-1], 'ctx', route)))  29.9 us
    pallas_call x2, Pallas kernels, norm_part(): pl.pallas_call(functools.partial(norm_kernel, chunk, image_rows, len(bloc...  25 us
    ppermute x12, starting transfers between devices, ring_blocks(): up = lax.ppermute(up, 'tp', ahead)  21.5 us
    pallas_call x2, Pallas kernels, back_part(): pl.pallas_call(functools.partial(back_kernel, chunk, image_rows, len(bloc...  13.5 us
    ppermute x8, waiting for transfers between devices, doubling_sum(): lax.ppermute(value, axis, [(t, t ^ bit) for t in range(count)])  12.1 us
  transfers between devices with their start and end apart: 49, of which 30 were waited for; matrix products, arithmetic and copies ran while one was open for 2% of the time, Pallas kernels for 21%

profile of v2, /device:TPU:0, one launch (start us, length us, event | category | flops | bytes accessed | tf_op | source)
XLA Modules:
  0.0 377.3 jit_solution(11777734815909935117)
XLA Ops:
  1.9 3.1 collective-permute-start.8
  5.0 11.9 %collective-permute-done.8.refs_1_ = bf16[512,512]{1,0:T(8,128)(2,1)S(1)} collective-permute-done((bf16[512,512]{1,0:T(8,128)(2,1)S(1)}, bf16[512,512]{1,0:T(8,128)(2,1)S(1)}, u32[]{:S(2)}, u32[]{:S(2)}) %collective-permute-start.8) | collective-permute-done | bytes 524320 | tf_op jit(solution)/shard_map/ppermute | solution.py:63
  16.9 1.8 collective-permute-start.10
  20.5 1.8 collective-permute-start
  22.5 9.3 %collective-permute-done.10.refs_3_ = bf16[512,512]{1,0:T(8,128)(2,1)} collective-permute-done((bf16[512,512]{1,0:T(8,128)(2,1)S(1)}, bf16[512,512]{1,0:T(8,128)(2,1)}, u32[]{:S(2)}, u32[]{:S(2)}) %collective-permute-start.10) | collective-permute-done | bytes 524320 | tf_op jit(solution)/shard_map/ppermute | solution.py:63
  31.8 1.8 collective-permute-start.12
  34.6 8.3 %collective-permute-done.refs_1_ = bf16[512,512]{1,0:T(8,128)(2,1)S(1)} collective-permute-done((bf16[512,512]{1,0:T(8,128)(2,1)S(1)}, bf16[512,512]{1,0:T(8,128)(2,1)S(1)}, u32[]{:S(2)}, u32[]{:S(2)}) %collective-permute-start) | collective-permute-done | bytes 524320 | tf_op jit(solution)/shard_map/ppermute | solution.py:63
  42.9 1.8 collective-permute-start.2
  46.5 7.6 %collective-permute-done.12.refs_5_ = bf16[512,512]{1,0:T(8,128)(2,1)S(1)} collective-permute-done((bf16[512,512]{1,0:T(8,128)(2,1)}, bf16[512,512]{1,0:T(8,128)(2,1)S(1)}, u32[]{:S(2)}, u32[]{:S(2)}) %collective-permute-start.12) | collective-permute-done | bytes 524320 | tf_op jit(solution)/shard_map/ppermute | solution.py:63
  54.2 1.8 collective-permute-start.14
  57.1 3.2 fusion.6
  60.2 5.2 %collective-permute-done.2.refs_3_ = bf16[512,512]{1,0:T(8,128)(2,1)S(1)} collective-permute-done((bf16[512,512]{1,0:T(8,128)(2,1)S(1)}, bf16[512,512]{1,0:T(8,128)(2,1)S(1)}, u32[]{:S(2)}, u32[]{:S(2)}) %collective-permute-start.2) | collective-permute-done | bytes 524320 | tf_op jit(solution)/shard_map/ppermute | solution.py:63
  65.4 1.8 collective-permute-start.4
  68.2 2.8 collective-permute-done.14.refs_7_
  71.0 2.6 collective-permute-done.15.refs_8_
  73.6 7.2 %shard_map.136 = (bf16[512,512]{1,0:T(8,128)(2,1)S(1)}, f32[1,512]{1,0:T(1,128)S(1)}, bf16[1024,4096]{1,0:T(8,128)(2,1)}, bf16[2048,1024]{1,0:T(8,128)(2,1)}) custom-call(s32[9]{0:T(128)S(1)} %pad_add_fusion.ring_ref, bf16[512,512]{1,0:T(8,128)(2,1)S(1)} %bitcast.43, bf16[512,512]{1,0:T(8,128)(2,1)S(1)} %copy-done.14, bf16[512,512]{1,0:T(8,128)(2,1)S(1)} %copy-done.16, ...), custom_call_target="tpu_custom_call" | custom-call | flops 2147483648 | bytes 12582912 | tf_op jit(solution)/shard_map/pallas_call | solution.py:164
  85.2 10.6 %collective-permute-done.19.refs_1_ = bf16[512,512]{1,0:T(8,128)(2,1)S(1)} collective-permute-done((bf16[512,512]{1,0:T(8,128)(2,1)S(1)}, bf16[512,512]{1,0:T(8,128)(2,1)S(1)}, u32[]{:S(2)}, u32[]{:S(2)}) %collective-permute-start.19) | collective-permute-done | bytes 524320 | tf_op jit(solution)/shard_map/ppermute | solution.py:63
  97.8 3.6 collective-permute-done.6.refs_7_
  102.9 6.3 %shard_map.137 = (bf16[512,512]{1,0:T(8,128)(2,1)S(1)}, f32[1,512]{1,0:T(1,128)S(1)}, bf16[1024,4096]{1,0:T(8,128)(2,1)}, bf16[2048,1024]{1,0:T(8,128)(2,1)}) custom-call(s32[9]{0:T(128)S(1)} %pad_add_fusion.ring_ref, bf16[512,512]{1,0:T(8,128)(2,1)S(1)} %bitcast.40, ...), custom_call_target="tpu_custom_call", output_to_operand_aliasing={{2}: (12, {}), {3}: (13, {})} | custom-call | flops 2147483648 | bytes 12582912 | tf_op jit(solution)/shard_map/pallas_call | solution.py:164
  114.6 9.5 %collective-permute-done.27.refs_1_ = bf16[512,512]{1,0:T(8,128)(2,1)S(1)} collective-permute-done((bf16[512,512]{1,0:T(8,128)(2,1)S(1)}, bf16[512,512]{1,0:T(8,128)(2,1)S(1)}, u32[]{:S(2)}, u32[]{:S(2)}) %collective-permute-start.27) | collective-permute-done | bytes 524320 | tf_op jit(solution)/shard_map/ppermute | solution.py:63
  126.2 9.2 %collective-permute-done.23.refs_5_ = bf16[512,512]{1,0:T(8,128)(2,1)S(1)} collective-permute-done((bf16[512,512]{1,0:T(8,128)(2,1)S(1)}, bf16[512,512]{1,0:T(8,128)(2,1)S(1)}, u32[]{:S(2)}, u32[]{:S(2)}) %collective-permute-start.23) | collective-permute-done | bytes 524320 | tf_op jit(solution)/shard_map/ppermute | solution.py:63
  137.8 8.8 %collective-permute-done.29.refs_3_ = bf16[512,512]{1,0:T(8,128)(2,1)S(1)} collective-permute-done((bf16[512,512]{1,0:T(8,128)(2,1)S(1)}, bf16[512,512]{1,0:T(8,128)(2,1)S(1)}, u32[]{:S(2)}, u32[]{:S(2)}) %collective-permute-start.29) | collective-permute-done | bytes 524320 | tf_op jit(solution)/shard_map/ppermute | solution.py:63
  148.7 3.6 collective-permute-done.25.refs_7_
  153.8 12.5 %shard_map.139 = (f32[1600,512]{1,0:T(8,128)}, f32[2,512]{1,0:T(2,128)S(1)}, f32[1600,128]{1,0:T(8,128)S(1)}, bf16[1024,4096]{1,0:T(8,128)(2,1)}, bf16[2048,1024]{1,0:T(8,128)(2,1)}) custom-call(s32[9]{0:T(128)S(1)} %pad_add_fusion.ring_ref, bf16[512,512]{1,0:T(8,128)(2,1)S(1)} %get-tuple-element.32.refs_0_, ...), custom_call_target="tpu_custom_call" | custom-call | flops 6710886400 | bytes 26411008 | tf_op jit(solution)/shard_map/pallas_call | solution.py:234
  167.6 3.2 collective-permute-done.35
  172.9 1.8 collective-permute-start.34
  174.7 1.7 collective-permute-start.37
  176.6 3.7 collective-permute-done.37
  180.4 12.5 %shard_map.140 = (f32[1600,512]{1,0:T(8,128)}, f32[2,512]{1,0:T(2,128)S(1)}, f32[1600,128]{1,0:T(8,128)S(1)}, bf16[1024,4096]{1,0:T(8,128)(2,1)}, bf16[2048,1024]{1,0:T(8,128)(2,1)}) custom-call(s32[9]{0:T(128)S(1)} %pad_add_fusion.ring_ref, bf16[512,512]{1,0:T(8,128)(2,1)S(1)} %get-tuple-element.34.refs_0_, ...), custom_call_target="tpu_custom_call", output_to_operand_aliasing={{3}: (16, {}), {4}: (17, {})} | custom-call | flops 6710886400 | bytes 26411008 | tf_op jit(solution)/shard_map/pallas_call | solution.py:234
  193.7 2.9 collective-permute-done.40
  197.9 2.3 collective-permute-done.41
  201.5 5.7 %shard_map.141.refs_0_ = bf16[8,1600,128]{2,1,0:T(8,128)(2,1)S(1)} custom-call(s32[8]{0:T(128)S(1)} %select_reduce_fusion.source_ref, s32[8]{0:T(128)S(1)} %convert_element_type.19.present_ref, f32[1600,512]{1,0:T(8,128)} %get-tuple-element.41.gained_ref, bf16[1600,1024]{1,0:T(8,128)(2,1)} %bitcast.32, f32[2,512]{1,0:T(2,128)S(1)} %add_multiply_fusion.2.refs_17_.means_ref, ...), custom_call_target="tpu_custom_call" | custom-call | flops 9830400 | bytes 13107200 | tf_op jit(solution)/shard_map/pallas_call | solution.py:374
  207.2 1.7 copy-done.3
  209.0 4.7 %all-to-all-start = ((bf16[8,1600,128]{2,1,0:T(8,128)(2,1)}), bf16[8,1600,128]{2,1,0:T(8,128)(2,1)}, u32[]{:S(2)}, u32[]{:S(2)}) async-start(bf16[8,1600,128]{2,1,0:T(8,128)(2,1)} %copy-done.3), calls=%async_computation | async-start | bytes 6553600 | tf_op jit(solution)/shard_map/all_to_all | solution.py:527
  214.3 5.6 %collective-permute-done.38.a_other_ref = bf16[1600,1024]{1,0:T(8,128)(2,1)} collective-permute-done((bf16[1600,1024]{1,0:T(8,128)(2,1)S(1)}, bf16[1600,1024]{1,0:T(8,128)(2,1)}, u32[]{:S(2)}, u32[]{:S(2)}) %collective-permute-start.38) | collective-permute-done | bytes 3276832 | tf_op jit(solution)/shard_map/ppermute | solution.py:426
  219.9 7.2 %shard_map.143 = bf16[800,1024]{1,0:T(8,128)(2,1)} custom-call(s32[1]{0:T(128)} %bitcast.6.member_ref, bf16[1600,1024]{1,0:T(8,128)(2,1)S(1)} %bitcast.36, bf16[1600,1024]{1,0:T(8,128)(2,1)} %collective-permute-done.38.a_other_ref, bf16[1024,4096]{1,0:T(8,128)(2,1)} %get-tuple-element.39.b_ref, bf16[2048,1024]{1,0:T(8,128)(2,1)} %collective-permute-done.39.b_other_ref, ...), custom_call_target="tpu_custom_call" | custom-call | flops 209715200 | bytes 466944 | tf_op jit(solution)/shard_map/pallas_call | solution.py:297
  228.6 5.7 %shard_map.148.refs_0_ = bf16[8,1600,128]{2,1,0:T(8,128)(2,1)S(1)} custom-call(s32[8]{0:T(128)S(1)} %select_reduce_fusion.source_ref, s32[8]{0:T(128)S(1)} %convert_element_type.19.present_ref, f32[1600,512]{1,0:T(8,128)} %get-tuple-element.44.gained_ref, bf16[1600,1024]{1,0:T(8,128)(2,1)} %bitcast.33, f32[2,512]{1,0:T(2,128)S(1)} %get-tuple-element.43.refs_0_.means_ref, ...), custom_call_target="tpu_custom_call" | custom-call | flops 9830400 | bytes 13107200 | tf_op jit(solution)/shard_map/pallas_call | solution.py:374
  234.2 53.9 %all-to-all-done.refs_2_ = bf16[8,1600,128]{2,1,0:T(8,128)(2,1)} async-done(((bf16[8,1600,128]{2,1,0:T(8,128)(2,1)}), bf16[8,1600,128]{2,1,0:T(8,128)(2,1)}, u32[]{:S(2)}, u32[]{:S(2)}) %all-to-all-start) | async-done | bytes 3276832 | tf_op jit(solution)/shard_map/all_to_all | solution.py:527
  289.9 4.7 %all-to-all-start.1 = ((bf16[8,1600,128]{2,1,0:T(8,128)(2,1)}), bf16[8,1600,128]{2,1,0:T(8,128)(2,1)}, u32[]{:S(2)}, u32[]{:S(2)}) async-start(bf16[8,1600,128]{2,1,0:T(8,128)(2,1)} %copy-done.2), calls=%async_computation.1 | async-start | bytes 6553600 | tf_op jit(solution)/shard_map/all_to_all | solution.py:558
  295.2 7.1 %shard_map.144 = bf16[800,1024]{1,0:T(8,128)(2,1)} custom-call(s32[1]{0:T(128)} %bitcast.6.member_ref, bf16[1600,1024]{1,0:T(8,128)(2,1)S(1)} %bitcast.37, bf16[1600,1024]{1,0:T(8,128)(2,1)} %collective-permute-done.38.a_other_ref, bf16[1024,4096]{1,0:T(8,128)(2,1)} %get-tuple-element.39.b_ref, bf16[2048,1024]{1,0:T(8,128)(2,1)} %collective-permute-done.39.b_other_ref, ...), custom_call_target="tpu_custom_call" | custom-call | flops 209715200 | bytes 466944 | tf_op jit(solution)/shard_map/pallas_call | solution.py:297
  303.8 2.0 copy-done.18
  305.9 5.7 %shard_map.138 = bf16[1024,512]{1,0:T(8,128)(2,1)} custom-call(s32[1]{0:T(128)} %bitcast.6.member_ref, bf16[1024,4096]{1,0:T(8,128)(2,1)} %get-tuple-element.28.a_ref, bf16[2048,1024]{1,0:T(8,128)(2,1)} %copy-done.18, bf16[1024,512]{1,0:T(8,128)(2,1)S(1)} %copy-done.4, bf16[1024,512]{1,0:T(8,128)(2,1)S(1)} %collective-permute-done.17.b_other_ref), custom_call_target="tpu_custom_call" | custom-call | flops 134217728 | bytes 393216 | tf_op jit(solution)/shard_map/pallas_call | solution.py:297
  313.5 27.6 %collective-permute-done.44.refs_2_.refs_1_ = bf16[800,1024]{1,0:T(8,128)(2,1)S(1)} collective-permute-done((bf16[800,1024]{1,0:T(8,128)(2,1)}, bf16[800,1024]{1,0:T(8,128)(2,1)S(1)}, u32[]{:S(2)}, u32[]{:S(2)}) %collective-permute-start.44) | collective-permute-done | bytes 1638432 | tf_op jit(solution)/shard_map/ppermute | solution.py:330
  341.2 5.6 %shard_map.150.refs_0_ = bf16[256,12800]{1,0:T(8,128)(2,1)} custom-call(bf16[12800,128]{1,0:T(8,128)(2,1)} %bitcast.17.in_ref), custom_call_target="tpu_custom_call" | custom-call | bytes 6553600 | tf_op jit(solution)/shard_map/pallas_call | solution.py:411
  348.3 12.4 %shard_map.147.refs_1_ = f32[1600,1024]{1,0:T(8,128)} custom-call(s32[1]{0:T(128)} %bitcast.member_ref, bf16[1600,1024]{1,0:T(8,128)(2,1)} %bitcast.34, bf16[1600,1024]{1,0:T(8,128)(2,1)} %collective-permute-done.38.a_other_ref, bf16[1024,4096]{1,0:T(8,128)(2,1)} %get-tuple-element.39.b_ref, bf16[2048,1024]{1,0:T(8,128)(2,1)} %collective-permute-done.39.b_other_ref, ...), custom_call_target="tpu_custom_call" | custom-call | flops 419430400 | bytes 671744 | tf_op jit(solution)/shard_map/pallas_call | solution.py:297
  360.8 2.3 collective-permute-done.18.refs_0_
  363.1 5.8 %shard_map.146.refs_2_ = f32[1024,512]{1,0:T(8,128)} custom-call(s32[1]{0:T(128)} %bitcast.member_ref, bf16[1024,4096]{1,0:T(8,128)(2,1)} %get-tuple-element.28.a_ref, bf16[2048,1024]{1,0:T(8,128)(2,1)} %copy-done.18, bf16[1024,512]{1,0:T(8,128)(2,1)S(1)} %copy-done.5, bf16[1024,512]{1,0:T(8,128)(2,1)S(1)} %copy-done.8, ...), custom_call_target="tpu_custom_call" | custom-call | flops 134217728 | bytes 393216 | tf_op jit(solution)/shard_map/pallas_call | solution.py:297
  371.7 5.6 %shard_map.151 = bf16[256,12800]{1,0:T(8,128)(2,1)} custom-call(bf16[12800,128]{1,0:T(8,128)(2,1)} %bitcast.16.in_ref, bf16[256,12800]{1,0:T(8,128)(2,1)} %shard_map.150.refs_0_, f32[1600,1024]{1,0:T(8,128)} %shard_map.147.refs_1_, f32[1024,512]{1,0:T(8,128)S(1)} %copy-done.6), custom_call_target="tpu_custom_call", output_to_operand_aliasing={{}: (1, {})} | custom-call | bytes 6553600 | tf_op jit(solution)/shard_map/pallas_call | solution.py:411
  (145 shorter events, 48.9 us)
Async XLA Ops:
  1.9 14.9 %collective-permute-start.8 = (bf16[512,512]{1,0:T(8,128)(2,1)S(1)}, bf16[512,512]{1,0:T(8,128)(2,1)S(1)}, u32[]{:S(2)}, u32[]{:S(2)}) collective-permute-start(bf16[512,512]{1,0:T(8,128)(2,1)S(1)} %bitcast.41), channel_id=1, source_target_pairs={{0,2},{2,4},{4,6},{6,7},{7,5},{5,3},{3,1},{1,0},{8,10},{10,12},{12... | collective-permute-start | bytes 1572872 | tf_op jit(solution)/shard_map/ppermute | solution.py:63
  5.0 14.5 %collective-permute-start.9 = (bf16[512,512]{1,0:T(8,128)(2,1)S(1)}, bf16[512,512]{1,0:T(8,128)(2,1)S(1)}, u32[]{:S(2)}, u32[]{:S(2)}) collective-permute-start(bf16[512,512]{1,0:T(8,128)(2,1)S(1)} %bitcast.42), channel_id=1, source_target_pairs={{0,1},{2,0},{4,2},{6,4},{7,6},{5,7},{3,5},{1,3},{8,9},{10,8},{12,1... | collective-permute-start | bytes 1572872 | tf_op jit(solution)/shard_map/ppermute | solution.py:64
  16.9 15.0 %collective-permute-start.10 = (bf16[512,512]{1,0:T(8,128)(2,1)S(1)}, bf16[512,512]{1,0:T(8,128)(2,1)}, u32[]{:S(2)}, u32[]{:S(2)}) collective-permute-start(bf16[512,512]{1,0:T(8,128)(2,1)S(1)} %collective-permute-done.8.refs_1_), channel_id=1, source_target_pairs={{0,2},{2,4},{4,6},{6,7},{7,5},{5,3},{3,1},{1,0},{8,10},{10,12},{12... | collective-permute-start | bytes 1572872 | tf_op jit(solution)/shard_map/ppermute | solution.py:63
  19.4 15.0 %collective-permute-start.11 = (bf16[512,512]{1,0:T(8,128)(2,1)S(1)}, bf16[512,512]{1,0:T(8,128)(2,1)}, u32[]{:S(2)}, u32[]{:S(2)}) collective-permute-start(bf16[512,512]{1,0:T(8,128)(2,1)S(1)} %collective-permute-done.9.refs_2_), channel_id=1, source_target_pairs={{0,1},{2,0},{4,2},{6,4},{7,6},{5,7},{3,5},{1,3},{8,9},{10,8},{12,1... | collective-permute-start | bytes 1572872 | tf_op jit(solution)/shard_map/ppermute | solution.py:64
  20.5 22.5 %collective-permute-start = (bf16[512,512]{1,0:T(8,128)(2,1)S(1)}, bf16[512,512]{1,0:T(8,128)(2,1)S(1)}, u32[]{:S(2)}, u32[]{:S(2)}) collective-permute-start(bf16[512,512]{1,0:T(8,128)(2,1)S(1)} %bitcast.38), channel_id=1, source_target_pairs={{0,2},{2,4},{4,6},{6,7},{7,5},{5,3},{3,1},{1,0},{8,10},{10,12},{12... | collective-permute-start | bytes 1572872 | tf_op jit(solution)/shard_map/ppermute | solution.py:63
  22.3 23.3 %collective-permute-start.1 = (bf16[512,512]{1,0:T(8,128)(2,1)S(1)}, bf16[512,512]{1,0:T(8,128)(2,1)S(1)}, u32[]{:S(2)}, u32[]{:S(2)}) collective-permute-start(bf16[512,512]{1,0:T(8,128)(2,1)S(1)} %bitcast.39), channel_id=1, source_target_pairs={{0,1},{2,0},{4,2},{6,4},{7,6},{5,7},{3,5},{1,3},{8,9},{10,8},{12,1... | collective-permute-start | bytes 1572872 | tf_op jit(solution)/shard_map/ppermute | solution.py:64
  31.8 22.4 %collective-permute-start.12 = (bf16[512,512]{1,0:T(8,128)(2,1)}, bf16[512,512]{1,0:T(8,128)(2,1)S(1)}, u32[]{:S(2)}, u32[]{:S(2)}) collective-permute-start(bf16[512,512]{1,0:T(8,128)(2,1)} %collective-permute-done.10.refs_3_), channel_id=1, source_target_pairs={{0,2},{2,4},{4,6},{6,7},{7,5},{5,3},{3,1},{1,0},{8,10},{10,12},{12... | collective-permute-start | bytes 1572872 | tf_op jit(solution)/shard_map/ppermute | solution.py:63
  34.4 22.4 %collective-permute-start.13 = (bf16[512,512]{1,0:T(8,128)(2,1)}, bf16[512,512]{1,0:T(8,128)(2,1)S(1)}, u32[]{:S(2)}, u32[]{:S(2)}) collective-permute-start(bf16[512,512]{1,0:T(8,128)(2,1)} %collective-permute-done.11.refs_4_), channel_id=1, source_target_pairs={{0,1},{2,0},{4,2},{6,4},{7,6},{5,7},{3,5},{1,3},{8,9},{10,8},{12,1... | collective-permute-start | bytes 1572872 | tf_op jit(solution)/shard_map/ppermute | solution.py:64
  42.9 22.5 %collective-permute-start.2 = (bf16[512,512]{1,0:T(8,128)(2,1)S(1)}, bf16[512,512]{1,0:T(8,128)(2,1)S(1)}, u32[]{:S(2)}, u32[]{:S(2)}) collective-permute-start(bf16[512,512]{1,0:T(8,128)(2,1)S(1)} %collective-permute-done.refs_1_), channel_id=1, source_target_pairs={{0,2},{2,4},{4,6},{6,7},{7,5},{5,3},{3,1},{1,0},{8,10},{10,12},{12... | collective-permute-start | bytes 1572872 | tf_op jit(solution)/shard_map/ppermute | solution.py:63
  45.5 22.5 %collective-permute-start.3 = (bf16[512,512]{1,0:T(8,128)(2,1)S(1)}, bf16[512,512]{1,0:T(8,128)(2,1)S(1)}, u32[]{:S(2)}, u32[]{:S(2)}) collective-permute-start(bf16[512,512]{1,0:T(8,128)(2,1)S(1)} %collective-permute-done.1.refs_2_), channel_id=1, source_target_pairs={{0,1},{2,0},{4,2},{6,4},{7,6},{5,7},{3,5},{1,3},{8,9},{10,8},{12,1... | collective-permute-start | bytes 1572872 | tf_op jit(solution)/shard_map/ppermute | solution.py:64
  54.2 16.8 %collective-permute-start.14 = (bf16[256,512]{1,0:T(8,128)(2,1)S(1)}, bf16[256,512]{1,0:T(8,128)(2,1)S(1)}, u32[]{:S(2)}, u32[]{:S(2)}) collective-permute-start(bf16[256,512]{1,0:T(8,128)(2,1)S(1)} %slice.60), channel_id=1, source_target_pairs={{0,2},{2,4},{4,6},{6,7},{7,5},{5,3},{3,1},{1,0},{8,10},{10,12},{12... | collective-permute-start | bytes 786440 | tf_op jit(solution)/shard_map/ppermute | solution.py:67
  56.8 16.8 %collective-permute-start.15 = (bf16[256,512]{1,0:T(8,128)(2,1)S(1)}, bf16[256,512]{1,0:T(8,128)(2,1)S(1)}, u32[]{:S(2)}, u32[]{:S(2)}) collective-permute-start(bf16[256,512]{1,0:T(8,128)(2,1)S(1)} %slice.61), channel_id=1, source_target_pairs={{0,1},{2,0},{4,2},{6,4},{7,6},{5,7},{3,5},{1,3},{8,9},{10,8},{12,1... | collective-permute-start | bytes 786440 | tf_op jit(solution)/shard_map/ppermute | solution.py:68
  65.4 17.5 %collective-permute-start.4 = (bf16[512,512]{1,0:T(8,128)(2,1)S(1)}, bf16[512,512]{1,0:T(8,128)(2,1)S(1)}, u32[]{:S(2)}, u32[]{:S(2)}) collective-permute-start(bf16[512,512]{1,0:T(8,128)(2,1)S(1)} %collective-permute-done.2.refs_3_), channel_id=1, source_target_pairs={{0,2},{2,4},{4,6},{6,7},{7,5},{5,3},{3,1},{1,0},{8,10},{10,12},{12... | collective-permute-start | bytes 1572872 | tf_op jit(solution)/shard_map/ppermute | solution.py:63
  68.0 16.8 %collective-permute-start.5 = (bf16[512,512]{1,0:T(8,128)(2,1)S(1)}, bf16[512,512]{1,0:T(8,128)(2,1)S(1)}, u32[]{:S(2)}, u32[]{:S(2)}) collective-permute-start(bf16[512,512]{1,0:T(8,128)(2,1)S(1)} %collective-permute-done.3.refs_4_), channel_id=1, source_target_pairs={{0,1},{2,0},{4,2},{6,4},{7,6},{5,7},{3,5},{1,3},{8,9},{10,8},{12,1... | collective-permute-start | bytes 1572872 | tf_op jit(solution)/shard_map/ppermute | solution.py:64
  80.8 14.9 %collective-permute-start.19 = (bf16[512,512]{1,0:T(8,128)(2,1)S(1)}, bf16[512,512]{1,0:T(8,128)(2,1)S(1)}, u32[]{:S(2)}, u32[]{:S(2)}) collective-permute-start(bf16[512,512]{1,0:T(8,128)(2,1)S(1)} %get-tuple-element.32.refs_0_), channel_id=1, source_target_pairs={{0,2},{2,4},{4,6},{6,7},{7,5},{5,3},{3,1},{1,0},{8,10},{10,12},{12... | collective-permute-start | bytes 1572872 | tf_op jit(solution)/shard_map/ppermute | solution.py:63
  82.5 14.9 %collective-permute-start.20 = (bf16[512,512]{1,0:T(8,128)(2,1)S(1)}, bf16[512,512]{1,0:T(8,128)(2,1)S(1)}, u32[]{:S(2)}, u32[]{:S(2)}) collective-permute-start(bf16[512,512]{1,0:T(8,128)(2,1)S(1)} %get-tuple-element.32.refs_0_), channel_id=1, source_target_pairs={{0,1},{2,0},{4,2},{6,4},{7,6},{5,7},{3,5},{1,3},{8,9},{10,8},{12,1... | collective-permute-start | bytes 1572872 | tf_op jit(solution)/shard_map/ppermute | solution.py:64
  82.9 18.4 %collective-permute-start.6 = (bf16[256,512]{1,0:T(8,128)(2,1)S(1)}, bf16[256,512]{1,0:T(8,128)(2,1)S(1)}, u32[]{:S(2)}, u32[]{:S(2)}) collective-permute-start(bf16[256,512]{1,0:T(8,128)(2,1)S(1)} %slice.57), channel_id=1, source_target_pairs={{0,2},{2,4},{4,6},{6,7},{7,5},{5,3},{3,1},{1,0},{8,10},{10,12},{12... | collective-permute-start | bytes 786440 | tf_op jit(solution)/shard_map/ppermute | solution.py:67
  84.8 18.1 %collective-permute-start.7 = (bf16[256,512]{1,0:T(8,128)(2,1)S(1)}, bf16[256,512]{1,0:T(8,128)(2,1)S(1)}, u32[]{:S(2)}, u32[]{:S(2)}) collective-permute-start(bf16[256,512]{1,0:T(8,128)(2,1)S(1)} %slice.58), channel_id=1, source_target_pairs={{0,1},{2,0},{4,2},{6,4},{7,6},{5,7},{3,5},{1,3},{8,9},{10,8},{12,1... | collective-permute-start | bytes 786440 | tf_op jit(solution)/shard_map/ppermute | solution.py:68
  95.7 16.5 %collective-permute-start.21 = (bf16[512,512]{1,0:T(8,128)(2,1)S(1)}, bf16[512,512]{1,0:T(8,128)(2,1)S(1)}, u32[]{:S(2)}, u32[]{:S(2)}) collective-permute-start(bf16[512,512]{1,0:T(8,128)(2,1)S(1)} %collective-permute-done.19.refs_1_), channel_id=1, source_target_pairs={{0,2},{2,4},{4,6},{6,7},{7,5},{5,3},{3,1},{1,0},{8,10},{10,12},{12... | collective-permute-start | bytes 1572872 | tf_op jit(solution)/shard_map/ppermute | solution.py:63
  97.3 16.8 %collective-permute-start.22 = (bf16[512,512]{1,0:T(8,128)(2,1)S(1)}, bf16[512,512]{1,0:T(8,128)(2,1)S(1)}, u32[]{:S(2)}, u32[]{:S(2)}) collective-permute-start(bf16[512,512]{1,0:T(8,128)(2,1)S(1)} %collective-permute-done.20.refs_2_), channel_id=1, source_target_pairs={{0,1},{2,0},{4,2},{6,4},{7,6},{5,7},{3,5},{1,3},{8,9},{10,8},{12,1... | collective-permute-start | bytes 1572872 | tf_op jit(solution)/shard_map/ppermute | solution.py:64
  109.2 14.9 %collective-permute-start.27 = (bf16[512,512]{1,0:T(8,128)(2,1)S(1)}, bf16[512,512]{1,0:T(8,128)(2,1)S(1)}, u32[]{:S(2)}, u32[]{:S(2)}) collective-permute-start(bf16[512,512]{1,0:T(8,128)(2,1)S(1)} %get-tuple-element.34.refs_0_), channel_id=1, source_target_pairs={{0,2},{2,4},{4,6},{6,7},{7,5},{5,3},{3,1},{1,0},{8,10},{10,12},{12... | collective-permute-start | bytes 1572872 | tf_op jit(solution)/shard_map/ppermute | solution.py:63
  110.9 14.9 %collective-permute-start.28 = (bf16[512,512]{1,0:T(8,128)(2,1)S(1)}, bf16[512,512]{1,0:T(8,128)(2,1)S(1)}, u32[]{:S(2)}, u32[]{:S(2)}) collective-permute-start(bf16[512,512]{1,0:T(8,128)(2,1)S(1)} %get-tuple-element.34.refs_0_), channel_id=1, source_target_pairs={{0,1},{2,0},{4,2},{6,4},{7,6},{5,7},{3,5},{1,3},{8,9},{10,8},{12,1... | collective-permute-start | bytes 1572872 | tf_op jit(solution)/shard_map/ppermute | solution.py:64
  112.3 23.1 %collective-permute-start.23 = (bf16[512,512]{1,0:T(8,128)(2,1)S(1)}, bf16[512,512]{1,0:T(8,128)(2,1)S(1)}, u32[]{:S(2)}, u32[]{:S(2)}) collective-permute-start(bf16[512,512]{1,0:T(8,128)(2,1)S(1)} %collective-permute-done.21.refs_3_), channel_id=1, source_target_pairs={{0,2},{2,4},{4,6},{6,7},{7,5},{5,3},{3,1},{1,0},{8,10},{10,12},{12... | collective-permute-start | bytes 1572872 | tf_op jit(solution)/shard_map/ppermute | solution.py:63
  114.2 22.9 %collective-permute-start.24 = (bf16[512,512]{1,0:T(8,128)(2,1)S(1)}, bf16[512,512]{1,0:T(8,128)(2,1)S(1)}, u32[]{:S(2)}, u32[]{:S(2)}) collective-permute-start(bf16[512,512]{1,0:T(8,128)(2,1)S(1)} %collective-permute-done.22.refs_4_), channel_id=1, source_target_pairs={{0,1},{2,0},{4,2},{6,4},{7,6},{5,7},{3,5},{1,3},{8,9},{10,8},{12,1... | collective-permute-start | bytes 1572872 | tf_op jit(solution)/shard_map/ppermute | solution.py:64
  124.2 22.5 %collective-permute-start.29 = (bf16[512,512]{1,0:T(8,128)(2,1)S(1)}, bf16[512,512]{1,0:T(8,128)(2,1)S(1)}, u32[]{:S(2)}, u32[]{:S(2)}) collective-permute-start(bf16[512,512]{1,0:T(8,128)(2,1)S(1)} %collective-permute-done.27.refs_1_), channel_id=1, source_target_pairs={{0,2},{2,4},{4,6},{6,7},{7,5},{5,3},{3,1},{1,0},{8,10},{10,12},{12... | collective-permute-start | bytes 1572872 | tf_op jit(solution)/shard_map/ppermute | solution.py:63
  125.7 22.5 %collective-permute-start.30 = (bf16[512,512]{1,0:T(8,128)(2,1)S(1)}, bf16[512,512]{1,0:T(8,128)(2,1)S(1)}, u32[]{:S(2)}, u32[]{:S(2)}) collective-permute-start(bf16[512,512]{1,0:T(8,128)(2,1)S(1)} %collective-permute-done.28.refs_2_), channel_id=1, source_target_pairs={{0,1},{2,0},{4,2},{6,4},{7,6},{5,7},{3,5},{1,3},{8,9},{10,8},{12,1... | collective-permute-start | bytes 1572872 | tf_op jit(solution)/shard_map/ppermute | solution.py:64
  135.4 16.8 %collective-permute-start.25 = (bf16[256,512]{1,0:T(8,128)(2,1)S(1)}, bf16[256,512]{1,0:T(8,128)(2,1)S(1)}, u32[]{:S(2)}, u32[]{:S(2)}) collective-permute-start(bf16[256,512]{1,0:T(8,128)(2,1)S(1)} %slice.62), channel_id=1, source_target_pairs={{0,2},{2,4},{4,6},{6,7},{7,5},{5,3},{3,1},{1,0},{8,10},{10,12},{12... | collective-permute-start | bytes 786440 | tf_op jit(solution)/shard_map/ppermute | solution.py:67
  137.1 16.8 %collective-permute-start.26 = (bf16[256,512]{1,0:T(8,128)(2,1)S(1)}, bf16[256,512]{1,0:T(8,128)(2,1)S(1)}, u32[]{:S(2)}, u32[]{:S(2)}) collective-permute-start(bf16[256,512]{1,0:T(8,128)(2,1)S(1)} %slice.63), channel_id=1, source_target_pairs={{0,1},{2,0},{4,2},{6,4},{7,6},{5,7},{3,5},{1,3},{8,9},{10,8},{12,1... | collective-permute-start | bytes 786440 | tf_op jit(solution)/shard_map/ppermute | solution.py:68
  146.6 25.7 %collective-permute-start.31 = (bf16[512,512]{1,0:T(8,128)(2,1)S(1)}, bf16[512,512]{1,0:T(8,128)(2,1)S(1)}, u32[]{:S(2)}, u32[]{:S(2)}) collective-permute-start(bf16[512,512]{1,0:T(8,128)(2,1)S(1)} %collective-permute-done.29.refs_3_), channel_id=1, source_target_pairs={{0,2},{2,4},{4,6},{6,7},{7,5},{5,3},{3,1},{1,0},{8,10},{10,12},{12... | collective-permute-start | bytes 1572872 | tf_op jit(solution)/shard_map/ppermute | solution.py:63
  148.2 24.7 %collective-permute-start.32 = (bf16[512,512]{1,0:T(8,128)(2,1)S(1)}, bf16[512,512]{1,0:T(8,128)(2,1)S(1)}, u32[]{:S(2)}, u32[]{:S(2)}) collective-permute-start(bf16[512,512]{1,0:T(8,128)(2,1)S(1)} %collective-permute-done.30.refs_4_), channel_id=1, source_target_pairs={{0,1},{2,0},{4,2},{6,4},{7,6},{5,7},{3,5},{1,3},{8,9},{10,8},{12,1... | collective-permute-start | bytes 1572872 | tf_op jit(solution)/shard_map/ppermute | solution.py:64
  170.8 3.9 %collective-permute-start.36 = (f32[2,512]{1,0:T(2,128)S(1)}, f32[2,512]{1,0:T(2,128)S(1)}, u32[]{:S(2)}, u32[]{:S(2)}) collective-permute-start(f32[2,512]{1,0:T(2,128)S(1)} %add.72), channel_id=1, source_target_pairs={{0,2},{1,3},{2,0},{3,1},{4,6},{5,7},{6,4},{7,5},{8,10},{9,11},{10,... | collective-permute-start | bytes 12296 | tf_op jit(solution)/shard_map/ppermute | solution.py:434
  172.4 8.0 %collective-permute-start.33 = (bf16[256,512]{1,0:T(8,128)(2,1)S(1)}, bf16[256,512]{1,0:T(8,128)(2,1)S(1)}, u32[]{:S(2)}, u32[]{:S(2)}) collective-permute-start(bf16[256,512]{1,0:T(8,128)(2,1)S(1)} %slice.64), channel_id=1, source_target_pairs={{0,2},{2,4},{4,6},{6,7},{7,5},{5,3},{3,1},{1,0},{8,10},{10,12},{12... | collective-permute-start | bytes 786440 | tf_op jit(solution)/shard_map/ppermute | solution.py:67
  172.9 7.4 %collective-permute-start.34 = (bf16[256,512]{1,0:T(8,128)(2,1)S(1)}, bf16[256,512]{1,0:T(8,128)(2,1)S(1)}, u32[]{:S(2)}, u32[]{:S(2)}) collective-permute-start(bf16[256,512]{1,0:T(8,128)(2,1)S(1)} %slice.65), channel_id=1, source_target_pairs={{0,1},{2,0},{4,2},{6,4},{7,6},{5,7},{3,5},{1,3},{8,9},{10,8},{12,1... | collective-permute-start | bytes 786440 | tf_op jit(solution)/shard_map/ppermute | solution.py:68
  174.7 5.6 %collective-permute-start.37 = (f32[2,512]{1,0:T(2,128)S(1)}, f32[2,512]{1,0:T(2,128)S(1)}, u32[]{:S(2)}, u32[]{:S(2)}) collective-permute-start(f32[2,512]{1,0:T(2,128)S(1)} %add.73), channel_id=1, source_target_pairs={{0,4},{1,5},{2,6},{3,7},{4,0},{5,1},{6,2},{7,3},{8,12},{9,13},{10,... | collective-permute-start | bytes 12296 | tf_op jit(solution)/shard_map/ppermute | solution.py:434
  192.9 3.7 collective-permute-start.40
  196.6 3.6 collective-permute-start.41
  200.2 7.0 %collective-permute-start.42 = (f32[2,512]{1,0:T(2,128)S(1)}, f32[2,512]{1,0:T(2,128)S(1)}, u32[]{:S(2)}, u32[]{:S(2)}) collective-permute-start(f32[2,512]{1,0:T(2,128)S(1)} %add.78), channel_id=1, source_target_pairs={{0,4},{1,5},{2,6},{3,7},{4,0},{5,1},{6,2},{7,3},{8,12},{9,13},{10,... | collective-permute-start | bytes 12296 | tf_op jit(solution)/shard_map/ppermute | solution.py:434
  201.4 18.5 %collective-permute-start.39 = (bf16[2048,1024]{1,0:T(8,128)(2,1)}, bf16[2048,1024]{1,0:T(8,128)(2,1)}, u32[]{:S(2)}, u32[]{:S(2)}) collective-permute-start(bf16[2048,1024]{1,0:T(8,128)(2,1)} %get-tuple-element.40), channel_id=1, source_target_pairs={{0,8},{8,0},{16,24},{24,16},{1,9},{9,1},{17,25},{25,17},{2,10},{10... | collective-permute-start | bytes 12582920 | tf_op jit(solution)/shard_map/ppermute | solution.py:426
  209.0 79.2 %all-to-all-start = ((bf16[8,1600,128]{2,1,0:T(8,128)(2,1)}), bf16[8,1600,128]{2,1,0:T(8,128)(2,1)}, u32[]{:S(2)}, u32[]{:S(2)}) async-start(bf16[8,1600,128]{2,1,0:T(8,128)(2,1)} %copy-done.3), calls=%async_computation | async-start | bytes 6553600 | tf_op jit(solution)/shard_map/all_to_all | solution.py:527
  213.7 6.2 %collective-permute-start.38 = (bf16[1600,1024]{1,0:T(8,128)(2,1)S(1)}, bf16[1600,1024]{1,0:T(8,128)(2,1)}, u32[]{:S(2)}, u32[]{:S(2)}) collective-permute-start(bf16[1600,1024]{1,0:T(8,128)(2,1)S(1)} %bitcast.35), channel_id=1, source_target_pairs={{0,8},{8,0},{16,24},{24,16},{1,9},{9,1},{17,25},{25,17},{2,10},{10... | collective-permute-start | bytes 9830408 | tf_op jit(solution)/shard_map/ppermute | solution.py:426
  227.1 61.1 %collective-permute-start.43 = (bf16[800,1024]{1,0:T(8,128)(2,1)}, bf16[800,1024]{1,0:T(8,128)(2,1)}, u32[]{:S(2)}, u32[]{:S(2)}) collective-permute-start(bf16[800,1024]{1,0:T(8,128)(2,1)} %shard_map.143), channel_id=1, source_target_pairs={{0,16},{8,24},{16,0},{24,8},{1,17},{9,25},{17,1},{25,9},{2,18},{10... | collective-permute-start | bytes 4915208 | tf_op jit(solution)/shard_map/ppermute | solution.py:330
  289.9 80.3 %all-to-all-start.1 = ((bf16[8,1600,128]{2,1,0:T(8,128)(2,1)}), bf16[8,1600,128]{2,1,0:T(8,128)(2,1)}, u32[]{:S(2)}, u32[]{:S(2)}) async-start(bf16[8,1600,128]{2,1,0:T(8,128)(2,1)} %copy-done.2), calls=%async_computation.1 | async-start | bytes 6553600 | tf_op jit(solution)/shard_map/all_to_all | solution.py:558
  294.6 9.2 %collective-permute-start.16 = (bf16[2048,1024]{1,0:T(8,128)(2,1)}, bf16[2048,1024]{1,0:T(8,128)(2,1)S(1)}, u32[]{:S(2)}, u32[]{:S(2)}) collective-permute-start(bf16[2048,1024]{1,0:T(8,128)(2,1)} %get-tuple-element.29), channel_id=1, source_target_pairs={{0,8},{8,0},{16,24},{24,16},{1,9},{9,1},{17,25},{25,17},{2,10},{10... | collective-permute-start | bytes 12582920 | tf_op jit(solution)/shard_map/ppermute | solution.py:426
  294.7 9.1 %collective-permute-start.17 = (bf16[1024,512]{1,0:T(8,128)(2,1)}, bf16[1024,512]{1,0:T(8,128)(2,1)S(1)}, u32[]{:S(2)}, u32[]{:S(2)}) collective-permute-start(bf16[1024,512]{1,0:T(8,128)(2,1)} %get-tuple-element.46.b_ref), channel_id=1, source_target_pairs={{0,8},{8,0},{16,24},{24,16},{1,9},{9,1},{17,25},{25,17},{2,10},{10... | collective-permute-start | bytes 3145736 | tf_op jit(solution)/shard_map/ppermute | solution.py:426
  302.3 38.9 %collective-permute-start.44 = (bf16[800,1024]{1,0:T(8,128)(2,1)}, bf16[800,1024]{1,0:T(8,128)(2,1)S(1)}, u32[]{:S(2)}, u32[]{:S(2)}) collective-permute-start(bf16[800,1024]{1,0:T(8,128)(2,1)} %shard_map.144), channel_id=1, source_target_pairs={{0,16},{8,24},{16,0},{24,8},{1,17},{9,25},{17,1},{25,9},{2,18},{10... | collective-permute-start | bytes 4915208 | tf_op jit(solution)/shard_map/ppermute | solution.py:330
  311.6 51.4 %collective-permute-start.18 = (bf16[1024,512]{1,0:T(8,128)(2,1)}, bf16[1024,512]{1,0:T(8,128)(2,1)S(1)}, u32[]{:S(2)}, u32[]{:S(2)}) collective-permute-start(bf16[1024,512]{1,0:T(8,128)(2,1)} %shard_map.138), channel_id=1, source_target_pairs={{0,16},{8,24},{16,0},{24,8},{1,17},{9,25},{17,1},{25,9},{2,18},{10... | collective-permute-start | bytes 3145736 | tf_op jit(solution)/shard_map/ppermute | solution.py:330
  341.2 5.6 %collective-permute-start.45 = (f32[4224]{0:T(1024)S(1)}, f32[4224]{0:T(1024)S(1)}, u32[]{:S(2)}, u32[]{:S(2)}) collective-permute-start(f32[4224]{0:T(1024)S(1)} %shard_map.145.refs_1_), channel_id=1, source_target_pairs={{0,8},{8,0},{16,24},{24,16},{1,9},{9,1},{17,25},{25,17},{2,10},{10... | collective-permute-start | bytes 50696 | tf_op jit(solution)/shard_map/ppermute | solution.py:434
  346.8 22.1 %collective-permute-start.46 = (f32[4224]{0:T(1024)S(1)}, f32[4224]{0:T(1024)S(1)}, u32[]{:S(2)}, u32[]{:S(2)}) collective-permute-start(f32[4224]{0:T(1024)S(1)} %add.80), channel_id=1, source_target_pairs={{0,16},{8,24},{16,0},{24,8},{1,17},{9,25},{17,1},{25,9},{2,18},{10... | collective-permute-start | bytes 50696 | tf_op jit(solution)/shard_map/ppermute | solution.py:434
  (23 other events, 263.6 us)
